TPU v7x, 32 devices: a whole 2x2x4 slice. The times are simulated.
32 devices in a mesh: groups: 2 (over y), section: 4 (over z), dp: 2 (over x), space: 2 (over core).
Axes of the slice: x: 2, y: 2, z: 4, core: 2. Of those that a mesh axis runs over, the one named last changes fastest.
Arguments:
- images: bfloat16 [8, 16, 16, 256], P(('groups', 'dp'), 'space'), parts along dimension 0, may hold values from -6 to 6
- timesteps: int32 [8], P(('groups', 'dp')), parts along dimension 0, may hold values from 0 to 999
- time_embed: float32 [1000, 256], replicated, may hold values from -3 to 3
- conv_weight: bfloat16 [4, 2, 2304, 256], P('section'), may hold values from -0.125 to 0.125
- norm_gain: float32 [4, 2, 256], P('section'), may hold values from 0.1 to 1.9
- out_grad: bfloat16 [8, 16, 16, 256], P(('groups', 'dp'), 'space'), parts along dimension 0, may hold values from -6 to 6
Outputs:
- weight_grad: float32 [8, 2, 2304, 256], P(('groups', 'section'), None, ('dp', 'space')), parts along dimension 0
There are 2 independent parts, one for each index of `groups`. A program takes and returns all parts, laid end to end along the dimension named above; an argument that names none is the same for every part. Nothing has to cross between parts.
All inputs are finite; a program needn't handle non-finite values.
Results may differ from a plain program's by a relative error of at most 0.013.
Values may be sent and summed in bfloat16 or wider, within the bound.
A program may use at most 64 MiB of HBM per device.

v0:
```python
import math

import jax
import jax.numpy as jnp
from jax import lax
from jax.sharding import PartitionSpec as P

EPSILON = 1e-06


def passed_along(value, axis, steps):
    count = lax.axis_size(axis)
    leading, last = (max(0, -steps), min(count, count - steps))
    return lax.ppermute(value, axis, [(source, source + steps) for source in range(leading, last)])


def padded_2(x, sides, width):
    for axis, dim in sides:
        size, length = (lax.axis_size(axis), x.shape[dim])
        up = [(i, (i + 1) % size) for i in range(size - 1)]
        down = [(j, i) for i, j in up]
        last = lax.slice_in_dim(x, length - width, length, axis=dim)
        leading = lax.slice_in_dim(x, 0, width, axis=dim)
        before = lax.ppermute(last, axis, up)
        after = lax.ppermute(leading, axis, down)
        x = jnp.concatenate([before, x, after], axis=dim)
    return x


def normalize(values_in, gain_row, modulation):
    mean_sq = jnp.mean(values_in * values_in, axis=-1, keepdims=True)
    return jax.nn.silu(values_in * lax.rsqrt(mean_sq + EPSILON) * (gain_row * modulation))


def conv_taps(padded):
    band_rows = padded.shape[-3] - 2
    band_cols = padded.shape[-2]
    widths = [(0, 0)] * (padded.ndim - 2) + [(1, 1), (0, 0)]
    framed = jnp.pad(padded, widths)
    tap_stack = [
        framed[..., row_off : row_off + band_rows, col_off : col_off + band_cols, :]
        for row_off in range(3)
        for col_off in range(3)
    ]
    return jnp.concatenate(tap_stack, axis=-1)


def fold_taps(grad_taps, channels):
    band_rows, band_cols = (grad_taps.shape[-3], grad_taps.shape[-2])
    leading = grad_taps.shape[:-3]
    pieces = grad_taps.reshape(leading + (band_rows, band_cols, 9, channels))
    folded = jnp.zeros(leading + (band_rows + 2, band_cols + 2, channels), jnp.float32)
    for tap_index in range(9):
        row_off, col_off = (tap_index // 3, tap_index % 3)
        widths = [(0, 0)] * len(leading) + [(row_off, 2 - row_off), (col_off, 2 - col_off), (0, 0)]
        folded = folded + jnp.pad(pieces[..., tap_index, :], widths)
    return folded[..., 1:-1, :]


def apply_conv(tap_stack, weight):
    flat_rows = tap_stack.reshape(-1, tap_stack.shape[-1])
    result = jnp.dot(flat_rows, weight, preferred_element_type=jnp.float32)
    return result.reshape(tap_stack.shape[:-1] + (weight.shape[-1],))


def block_forward(a_pad, v_pad, weights, norm_gains, modulation, gated):
    f_main = normalize(a_pad.astype(jnp.float32), norm_gains[0], modulation).astype(jnp.bfloat16)
    f_side = normalize(v_pad.astype(jnp.float32), norm_gains[1], modulation).astype(jnp.bfloat16)
    p_main = apply_conv(conv_taps(f_main), weights[0])
    q_side = apply_conv(conv_taps(f_side), weights[1])
    centre = a_pad[..., 1:-1, :, :].astype(jnp.float32)
    mixed = jnp.where(gated, centre + p_main * jax.nn.sigmoid(q_side), centre + p_main + q_side)
    return (mixed.astype(jnp.bfloat16), p_main, q_side)


def block_backward(grad_out, a_pad, v_pad, p_main, q_side, weights, norm_gains, modulation, gated):
    f_main, pull_main = jax.vjp(
        lambda field_in: normalize(field_in, norm_gains[0], modulation), a_pad.astype(jnp.float32)
    )
    f_side, pull_side = jax.vjp(
        lambda field_in: normalize(field_in, norm_gains[1], modulation), v_pad.astype(jnp.float32)
    )
    taps_main = conv_taps(f_main.astype(jnp.bfloat16))
    taps_side = conv_taps(f_side.astype(jnp.bfloat16))
    gate_sig = jax.nn.sigmoid(q_side)
    back_main = jnp.where(gated, grad_out * gate_sig, grad_out).astype(jnp.bfloat16)
    back_side = jnp.where(gated, grad_out * p_main * gate_sig * (1.0 - gate_sig), grad_out).astype(
        jnp.bfloat16
    )
    channels = grad_out.shape[-1]
    grad_main = pull_main(fold_taps(apply_conv(back_main, weights[0].T), channels))[0]
    grad_side = pull_side(fold_taps(apply_conv(back_side, weights[1].T), channels))[0]
    widths = [(0, 0)] * (grad_out.ndim - 3) + [(1, 1), (0, 0), (0, 0)]
    grad_main = grad_main + jnp.pad(grad_out, widths)
    grad_input = jnp.where(gated, grad_main + grad_side, grad_main)
    grad_skip = jnp.where(gated, jnp.zeros_like(grad_side), grad_side)
    return (grad_input, grad_skip, taps_main, back_main, taps_side, back_side)


def move_bands(blocks, hops):
    return jnp.stack([passed_along(block, "section", hop) for block, hop in zip(blocks, hops)])


def rim_halo(stacked):
    return padded_2(stacked, (("space", 1),), 1)


def routed_forward(output):
    framed_all = rim_halo(move_bands((output, output, output), (2, -2, 1)))
    return (framed_all[0], framed_all[1], framed_all[2])


def routed_backward(grad_input, to_pair):
    moved = move_bands(
        (
            grad_input.astype(jnp.bfloat16),
            grad_input.astype(jnp.bfloat16),
            to_pair.astype(jnp.bfloat16),
        ),
        (2, -2, -1),
    )
    edges = jnp.concatenate([moved[:, :1], moved[:, -1:]], axis=1)
    beside_all = rim_halo(edges)
    centre = moved[:, 1:-1].astype(jnp.float32)
    band_rows = centre.shape[1]
    centre = centre + jnp.pad(
        beside_all[:, :1].astype(jnp.float32), ((0, 0), (0, band_rows - 1), (0, 0), (0, 0))
    )
    centre = centre + jnp.pad(
        beside_all[:, -1:].astype(jnp.float32), ((0, 0), (band_rows - 1, 0), (0, 0), (0, 0))
    )
    return (centre[0], centre[1], centre[2])


def shards(images, timesteps, time_embed, conv_weight, norm_gain, out_grad):
    micro_count, band_rows, band_cols, channels = images.shape
    sections = lax.axis_size("section")
    spaces = lax.axis_size("space")
    replicas = lax.axis_size("dp")
    section_index = lax.axis_index("section")
    is_encoder = section_index % 2 == 0
    block_index = section_index // 2
    position = jnp.where(is_encoder, block_index, sections - 1 - block_index)
    reverse = sections - 1 - position
    weights = conv_weight[0]
    norm_gains = norm_gain[0]
    table_rows = jnp.arange(time_embed.shape[0], dtype=jnp.int32)
    one_hot = (timesteps[:, None] == table_rows[None, :]).astype(jnp.float32)
    modulations = 1.0 + jnp.dot(one_hot, time_embed, precision=lax.Precision.HIGHEST)
    framed = padded_2(images, (("space", 1),), 1)
    tick_count = micro_count + sections - 1
    pad_block = jnp.zeros((band_rows + 2, band_cols, channels), jnp.bfloat16)
    store_pad = jnp.zeros((micro_count, band_rows + 2, band_cols, channels), jnp.bfloat16)
    store_pq = jnp.zeros((micro_count, 2, band_rows, band_cols, channels), jnp.float32)

    def forward_tick(tick_now, state_now):
        from_prev, from_next, from_pair, skip_store, input_store, pq_store = state_now
        skip_micro = tick_now - 1 - block_index
        take_skip = jnp.logical_and(
            jnp.logical_not(is_encoder), jnp.logical_and(skip_micro >= 0, skip_micro < micro_count)
        )
        skip_slot = jnp.clip(skip_micro, 0, micro_count - 1)
        skip_store = jnp.where(
            take_skip,
            lax.dynamic_update_index_in_dim(skip_store, from_pair, skip_slot, 0),
            skip_store,
        )
        micro_now = tick_now - position
        active = jnp.logical_and(micro_now >= 0, micro_now < micro_count)
        micro_slot = jnp.clip(micro_now, 0, micro_count - 1)
        input_pad = lax.dynamic_index_in_dim(framed, micro_slot, 0, keepdims=False)
        a_pad = jnp.where(
            section_index == 0,
            input_pad,
            jnp.where(
                section_index == sections - 1,
                from_pair,
                jnp.where(is_encoder, from_prev, from_next),
            ),
        )
        v_pad = jnp.where(
            is_encoder, a_pad, lax.dynamic_index_in_dim(skip_store, micro_slot, 0, keepdims=False)
        )
        modulation = lax.dynamic_index_in_dim(modulations, micro_slot, 0, keepdims=False)

        def forward_compute(operands):
            return block_forward(
                operands[0], operands[1], weights, norm_gains, operands[2], is_encoder
            )

        def forward_skipped(operands):
            empty = jnp.zeros((band_rows, band_cols, channels), jnp.float32)
            return (empty.astype(jnp.bfloat16), empty, empty)

        output, p_main, q_side = lax.cond(
            active, forward_compute, forward_skipped, (a_pad, v_pad, modulation)
        )
        input_store = jnp.where(
            active, lax.dynamic_update_index_in_dim(input_store, a_pad, micro_slot, 0), input_store
        )
        pq_store = jnp.where(
            active,
            lax.dynamic_update_index_in_dim(pq_store, jnp.stack([p_main, q_side]), micro_slot, 0),
            pq_store,
        )
        from_prev, from_next, from_pair = routed_forward(output)
        return (from_prev, from_next, from_pair, skip_store, input_store, pq_store)

    state_now = (pad_block, pad_block, pad_block, store_pad, store_pad, store_pq)
    state_now = lax.fori_loop(0, tick_count, forward_tick, state_now)
    skip_store, input_store, pq_store = (state_now[3], state_now[4], state_now[5])
    loss_scale = 1.0 / math.sqrt(micro_count * replicas * band_rows * spaces * band_cols)
    grad_block = jnp.zeros((band_rows, band_cols, channels), jnp.float32)
    gskip_start = jnp.zeros((micro_count, band_rows, band_cols, channels), jnp.float32)
    terms_start = jnp.zeros((2,) + weights.shape[1:], jnp.float32)

    def backward_tick(tick_now, state_now):
        from_prev, from_next, from_pair, gskip_store, weight_terms = state_now
        skip_micro = tick_now - 1 - block_index
        take_skip = jnp.logical_and(
            is_encoder, jnp.logical_and(skip_micro >= 0, skip_micro < micro_count)
        )
        skip_slot = jnp.clip(skip_micro, 0, micro_count - 1)
        gskip_store = jnp.where(
            take_skip,
            lax.dynamic_update_index_in_dim(gskip_store, from_pair, skip_slot, 0),
            gskip_store,
        )
        micro_now = tick_now - reverse
        active = jnp.logical_and(micro_now >= 0, micro_now < micro_count)
        micro_slot = jnp.clip(micro_now, 0, micro_count - 1)
        seed_grad = (
            lax.dynamic_index_in_dim(out_grad, micro_slot, 0, keepdims=False).astype(jnp.float32)
            * loss_scale
        )
        skip_part = lax.dynamic_index_in_dim(gskip_store, micro_slot, 0, keepdims=False)
        upstream = jnp.where(
            section_index == 1, seed_grad, jnp.where(is_encoder, from_next + skip_part, from_prev)
        )
        a_pad = lax.dynamic_index_in_dim(input_store, micro_slot, 0, keepdims=False)
        v_pad = jnp.where(
            is_encoder, a_pad, lax.dynamic_index_in_dim(skip_store, micro_slot, 0, keepdims=False)
        )
        pq_pair = lax.dynamic_index_in_dim(pq_store, micro_slot, 0, keepdims=False)
        modulation = lax.dynamic_index_in_dim(modulations, micro_slot, 0, keepdims=False)

        def backward_compute(operands):
            grad_input, grad_skip, taps_main, back_main, taps_side, back_side = block_backward(
                operands[0],
                operands[1],
                operands[2],
                operands[3][0],
                operands[3][1],
                weights,
                norm_gains,
                operands[4],
                is_encoder,
            )
            term_main = jnp.dot(
                taps_main.reshape(-1, taps_main.shape[-1]).T,
                back_main.reshape(-1, channels),
                preferred_element_type=jnp.float32,
            )
            term_side = jnp.dot(
                taps_side.reshape(-1, taps_side.shape[-1]).T,
                back_side.reshape(-1, channels),
                preferred_element_type=jnp.float32,
            )
            return (grad_input, grad_skip, jnp.stack([term_main, term_side]))

        def backward_skipped(operands):
            empty = jnp.zeros((band_rows + 2, band_cols, channels), jnp.float32)
            return (empty, empty, jnp.zeros_like(weight_terms))

        grad_input, grad_skip, step_terms = lax.cond(
            active,
            backward_compute,
            backward_skipped,
            (upstream, a_pad, v_pad, pq_pair, modulation),
        )
        weight_terms = weight_terms + step_terms
        to_pair = grad_skip + jnp.where(
            section_index == sections - 1, grad_input, jnp.zeros_like(grad_input)
        )
        from_prev, from_next, from_pair = routed_backward(grad_input, to_pair)
        return (from_prev, from_next, from_pair, gskip_store, weight_terms)

    state_back = (grad_block, grad_block, grad_block, gskip_start, terms_start)
    state_back = lax.fori_loop(0, tick_count, backward_tick, state_back)
    weight_terms = state_back[4]
    shares = lax.psum_scatter(
        weight_terms.astype(jnp.bfloat16), ("dp", "space"), scatter_dimension=1, tiled=True
    ).astype(jnp.float32)
    return shares[None]


def solution(mesh):
    placed = (
        P(("groups", "dp"), "space", None, None),
        P(("groups", "dp")),
        P(),
        P("section", None, None, None),
        P("section", None, None),
        P(("groups", "dp"), "space", None, None),
    )
    return jax.shard_map(
        shards,
        mesh=mesh,
        in_specs=placed,
        out_specs=P(("groups", "section"), None, ("dp", "space"), None),
        check_vma=False,
    )
```

profile of v0, /device:TPU:1, one launch (start us, length us, event | category | flops | bytes accessed | tf_op | source)
XLA Modules:
  0.0 378.3 jit_solution(16821525679309731139)
XLA Ops:
  8.9 3.0 collective-permute-start.11
  18.1 134.9 %while.49 = (s32[]{:T(128)}, bf16[10,16,256]{2,1,0:T(8,128)(2,1)}, bf16[10,16,256]{2,1,0:T(8,128)(2,1)}, bf16[10,16,256]{2,1,0:T(8,128)(2,1)}, bf16[2,10,16,256]...) while((s32[]{:T(128)}, bf16[10,16,256]{2,1,0:T(8,128)(2,1)}, ...), condition=%wide.region_5.6_spmd, body=%wide.region_0.5_spmd.sunk | while | flops 304177984 | bytes 11771084 | solution.py:210
  19.8 4.8 %conditional.5 = (bf16[8,16,256]{2,1,0:T(8,128)(2,1)S(1)}, f32[1,8,16,256]{3,2,1,0:T(8,128)}, f32[1,8,16,256]{3,2,1,0:T(8,128)S(1)}) conditional(s32[]{:T(128)} %convert_element_type.285, () %tuple.172, (pred[]{:T(512)}, bf16[10,16,256]{2,1,0:T(8,128)(2,1)S(1)}, f32[2,256]{1,0:T(2,128)S(1)}, f32[2,256]{1,0:T(2,128)S(1)}, s32[]{:T(128)}, ...), branch_computations={%region_1.1_spmd, %region_2.4_spmd} | conditional | flops 303301440 | bytes 7204901 | solution.py:195
  27.2 4.9 %collective-permute-start.2 = (bf16[8,16,256]{2,1,0:T(8,128)(2,1)S(1)}, bf16[8,16,256]{2,1,0:T(8,128)(2,1)S(1)}, u32[]{:S(2)}, u32[]{:S(2)}) collective-permute-start(bf16[8,16,256]{2,1,0:T(8,128)(2,1)S(1)} %get-tuple-element.1492), channel_id=1, source_target_pairs={{0,8},{4,12},{1,9},{5,13},{2,10},{6,14},{3,11},{7,15},{16,24},{20,... | collective-permute-start | bytes 196616 | tf_op jit(solution)/shard_map/while/body/eval_jaxpr/ppermute | solution.py:14
  34.6 3.2 collective-permute-start.3
  44.6 4.8 %conditional.5 = (bf16[8,16,256]{2,1,0:T(8,128)(2,1)S(1)}, f32[1,8,16,256]{3,2,1,0:T(8,128)}, f32[1,8,16,256]{3,2,1,0:T(8,128)S(1)}) conditional(s32[]{:T(128)} %convert_element_type.285, () %tuple.172, (pred[]{:T(512)}, bf16[10,16,256]{2,1,0:T(8,128)(2,1)S(1)}, f32[2,256]{1,0:T(2,128)S(1)}, f32[2,256]{1,0:T(2,128)S(1)}, s32[]{:T(128)}, ...), branch_computations={%region_1.1_spmd, %region_2.4_spmd} | conditional | flops 303301440 | bytes 7204901 | solution.py:195
  51.9 5.6 %collective-permute-start.2 = (bf16[8,16,256]{2,1,0:T(8,128)(2,1)S(1)}, bf16[8,16,256]{2,1,0:T(8,128)(2,1)S(1)}, u32[]{:S(2)}, u32[]{:S(2)}) collective-permute-start(bf16[8,16,256]{2,1,0:T(8,128)(2,1)S(1)} %get-tuple-element.1492), channel_id=1, source_target_pairs={{0,8},{4,12},{1,9},{5,13},{2,10},{6,14},{3,11},{7,15},{16,24},{20,... | collective-permute-start | bytes 196616 | tf_op jit(solution)/shard_map/while/body/eval_jaxpr/ppermute | solution.py:14
  59.5 4.7 %collective-permute-start.3 = (bf16[3,1,16,256]{3,2,1,0:T(8,128)(2,1)}, bf16[3,1,16,256]{3,2,1,0:T(8,128)(2,1)}, u32[]{:S(2)}, u32[]{:S(2)}) collective-permute-start(bf16[3,1,16,256]{3,2,1,0:T(8,128)(2,1)} %get-tuple-element.1493), channel_id=1, source_target_pairs={{1,0},{3,2},{5,4},{7,6},{9,8},{11,10},{13,12},{15,14},{17,16},{19,... | collective-permute-start | bytes 73736 | tf_op jit(solution)/shard_map/while/body/eval_jaxpr/ppermute | solution.py:25
  71.7 5.7 %collective-permute-start = (bf16[8,16,256]{2,1,0:T(8,128)(2,1)S(1)}, bf16[8,16,256]{2,1,0:T(8,128)(2,1)S(1)}, u32[]{:S(2)}, u32[]{:S(2)}) collective-permute-start(bf16[8,16,256]{2,1,0:T(8,128)(2,1)S(1)} %get-tuple-element.1492), channel_id=1, source_target_pairs={{0,4},{4,8},{8,12},{1,5},{5,9},{9,13},{2,6},{6,10},{10,14},{3,7},{... | collective-permute-start | bytes 196616 | tf_op jit(solution)/shard_map/while/body/eval_jaxpr/ppermute | solution.py:14
  78.7 9.0 %collective-permute-start.2 = (bf16[8,16,256]{2,1,0:T(8,128)(2,1)S(1)}, bf16[8,16,256]{2,1,0:T(8,128)(2,1)S(1)}, u32[]{:S(2)}, u32[]{:S(2)}) collective-permute-start(bf16[8,16,256]{2,1,0:T(8,128)(2,1)S(1)} %get-tuple-element.1492), channel_id=1, source_target_pairs={{0,8},{4,12},{1,9},{5,13},{2,10},{6,14},{3,11},{7,15},{16,24},{20,... | collective-permute-start | bytes 196616 | tf_op jit(solution)/shard_map/while/body/eval_jaxpr/ppermute | solution.py:14
  89.7 4.9 %collective-permute-start.3 = (bf16[3,1,16,256]{3,2,1,0:T(8,128)(2,1)}, bf16[3,1,16,256]{3,2,1,0:T(8,128)(2,1)}, u32[]{:S(2)}, u32[]{:S(2)}) collective-permute-start(bf16[3,1,16,256]{3,2,1,0:T(8,128)(2,1)} %get-tuple-element.1493), channel_id=1, source_target_pairs={{1,0},{3,2},{5,4},{7,6},{9,8},{11,10},{13,12},{15,14},{17,16},{19,... | collective-permute-start | bytes 73736 | tf_op jit(solution)/shard_map/while/body/eval_jaxpr/ppermute | solution.py:25
  102.1 5.8 %collective-permute-start = (bf16[8,16,256]{2,1,0:T(8,128)(2,1)S(1)}, bf16[8,16,256]{2,1,0:T(8,128)(2,1)S(1)}, u32[]{:S(2)}, u32[]{:S(2)}) collective-permute-start(bf16[8,16,256]{2,1,0:T(8,128)(2,1)S(1)} %get-tuple-element.1492), channel_id=1, source_target_pairs={{0,4},{4,8},{8,12},{1,5},{5,9},{9,13},{2,6},{6,10},{10,14},{3,7},{... | collective-permute-start | bytes 196616 | tf_op jit(solution)/shard_map/while/body/eval_jaxpr/ppermute | solution.py:14
  109.2 4.9 %collective-permute-start.2 = (bf16[8,16,256]{2,1,0:T(8,128)(2,1)S(1)}, bf16[8,16,256]{2,1,0:T(8,128)(2,1)S(1)}, u32[]{:S(2)}, u32[]{:S(2)}) collective-permute-start(bf16[8,16,256]{2,1,0:T(8,128)(2,1)S(1)} %get-tuple-element.1492), channel_id=1, source_target_pairs={{0,8},{4,12},{1,9},{5,13},{2,10},{6,14},{3,11},{7,15},{16,24},{20,... | collective-permute-start | bytes 196616 | tf_op jit(solution)/shard_map/while/body/eval_jaxpr/ppermute | solution.py:14
  116.1 5.2 %collective-permute-start.3 = (bf16[3,1,16,256]{3,2,1,0:T(8,128)(2,1)}, bf16[3,1,16,256]{3,2,1,0:T(8,128)(2,1)}, u32[]{:S(2)}, u32[]{:S(2)}) collective-permute-start(bf16[3,1,16,256]{3,2,1,0:T(8,128)(2,1)} %get-tuple-element.1493), channel_id=1, source_target_pairs={{1,0},{3,2},{5,4},{7,6},{9,8},{11,10},{13,12},{15,14},{17,16},{19,... | collective-permute-start | bytes 73736 | tf_op jit(solution)/shard_map/while/body/eval_jaxpr/ppermute | solution.py:25
  128.8 5.7 %collective-permute-start = (bf16[8,16,256]{2,1,0:T(8,128)(2,1)S(1)}, bf16[8,16,256]{2,1,0:T(8,128)(2,1)S(1)}, u32[]{:S(2)}, u32[]{:S(2)}) collective-permute-start(bf16[8,16,256]{2,1,0:T(8,128)(2,1)S(1)} %get-tuple-element.1492), channel_id=1, source_target_pairs={{0,4},{4,8},{8,12},{1,5},{5,9},{9,13},{2,6},{6,10},{10,14},{3,7},{... | collective-permute-start | bytes 196616 | tf_op jit(solution)/shard_map/while/body/eval_jaxpr/ppermute | solution.py:14
  135.9 4.9 %collective-permute-start.2 = (bf16[8,16,256]{2,1,0:T(8,128)(2,1)S(1)}, bf16[8,16,256]{2,1,0:T(8,128)(2,1)S(1)}, u32[]{:S(2)}, u32[]{:S(2)}) collective-permute-start(bf16[8,16,256]{2,1,0:T(8,128)(2,1)S(1)} %get-tuple-element.1492), channel_id=1, source_target_pairs={{0,8},{4,12},{1,9},{5,13},{2,10},{6,14},{3,11},{7,15},{16,24},{20,... | collective-permute-start | bytes 196616 | tf_op jit(solution)/shard_map/while/body/eval_jaxpr/ppermute | solution.py:14
  142.7 5.2 %collective-permute-start.3 = (bf16[3,1,16,256]{3,2,1,0:T(8,128)(2,1)}, bf16[3,1,16,256]{3,2,1,0:T(8,128)(2,1)}, u32[]{:S(2)}, u32[]{:S(2)}) collective-permute-start(bf16[3,1,16,256]{3,2,1,0:T(8,128)(2,1)} %get-tuple-element.1493), channel_id=1, source_target_pairs={{1,0},{3,2},{5,4},{7,6},{9,8},{11,10},{13,12},{15,14},{17,16},{19,... | collective-permute-start | bytes 73736 | tf_op jit(solution)/shard_map/while/body/eval_jaxpr/ppermute | solution.py:25
  155.8 175.6 %while.50 = (s32[]{:T(128)}, f32[8,16,256]{2,1,0:T(8,128)}, f32[8,16,256]{2,1,0:T(8,128)}, f32[8,16,256]{2,1,0:T(8,128)}, f32[2,8,16,256]{3,2,1,0:T(8,128)}, /*i...) while((s32[]{:T(128)}, f32[8,16,256]{2,1,0:T(8,128)}, ...), condition=%wide.region_13.14_spmd.clone, body=%wide.region_6.13_spmd.clone.sunk | while | flops 612088192 | bytes 57569524 | solution.py:289
  157.4 4.5 %conditional.6 = (f32[10,16,256]{2,1,0:T(8,128)}, f32[10,16,256]{2,1,0:T(8,128)}, f32[2,2304,256]{2,1,0:T(8,128)}, bf16[10,16,256]{2,1,0:T(8,128)(2,1)}) conditional(s32[]{:T(128)} %convert_element_type.288, () %tuple.177, (pred[]{:T(512)}, pred[]{:T(512)}, s32[]{:T(128)}, bf16[2,8,16,256]{3,2,1,0:T(8,128)(2,1)}, f32[2,8,16,256]{3,2,1,0:T(8,128)}, ...), branch_computations={%region_7.7_spmd, %region_8.12_spmd} | conditional | flops 608786816 | bytes 39218820 | solution.py:275
  157.4 2.5 broadcast.218
  163.2 6.1 %collective-permute-start.7 = (bf16[10,16,256]{2,1,0:T(8,128)(2,1)}, bf16[10,16,256]{2,1,0:T(8,128)(2,1)}, u32[]{:S(2)}, u32[]{:S(2)}) collective-permute-start(bf16[10,16,256]{2,1,0:T(8,128)(2,1)} %get-tuple-element.1521), channel_id=1, source_target_pairs={{0,8},{4,12},{1,9},{5,13},{2,10},{6,14},{3,11},{7,15},{16,24},{20,... | collective-permute-start | bytes 245768 | tf_op jit(solution)/shard_map/while/body/eval_jaxpr/ppermute | solution.py:14
  172.2 5.1 %select_add_fusion.2 = f32[2,2304,256]{2,1,0:T(8,128)} fusion(f32[2,2304,256]{2,1,0:T(8,128)} %get-tuple-element.1527, f32[2,2304,256]{2,1,0:T(8,128)} %get-tuple-element.1632, pred[]{:T(512)S(6)} %compare.31), kind=kLoop, calls=%fused_computation.218.clone.1 | loop fusion | flops 2359296 | bytes 14155777 | tf_op jit(solution)/shard_map/while/body/eval_jaxpr/add | solution.py:281
  177.3 2.3 collective-permute-done.5
  180.4 4.7 %collective-permute-start.8 = (bf16[3,1,16,256]{3,2,1,0:T(8,128)(2,1)S(1)}, bf16[3,1,16,256]{3,2,1,0:T(8,128)(2,1)S(1)}, u32[]{:S(2)}, u32[]{:S(2)}) collective-permute-start(bf16[3,1,16,256]{3,2,1,0:T(8,128)(2,1)S(1)} %get-tuple-element.1522), channel_id=1, source_target_pairs={{1,0},{3,2},{5,4},{7,6},{9,8},{11,10},{13,12},{15,14},{17,16},{19,... | collective-permute-start | bytes 73736 | tf_op jit(solution)/shard_map/while/body/eval_jaxpr/ppermute | solution.py:25
  190.6 4.5 %conditional.6 = (f32[10,16,256]{2,1,0:T(8,128)}, f32[10,16,256]{2,1,0:T(8,128)}, f32[2,2304,256]{2,1,0:T(8,128)}, bf16[10,16,256]{2,1,0:T(8,128)(2,1)}) conditional(s32[]{:T(128)} %convert_element_type.288, () %tuple.177, (pred[]{:T(512)}, pred[]{:T(512)}, s32[]{:T(128)}, bf16[2,8,16,256]{3,2,1,0:T(8,128)(2,1)}, f32[2,8,16,256]{3,2,1,0:T(8,128)}, ...), branch_computations={%region_7.7_spmd, %region_8.12_spmd} | conditional | flops 608786816 | bytes 39218820 | solution.py:275
  190.6 2.5 broadcast.218
  196.4 6.7 %collective-permute-start.7 = (bf16[10,16,256]{2,1,0:T(8,128)(2,1)}, bf16[10,16,256]{2,1,0:T(8,128)(2,1)}, u32[]{:S(2)}, u32[]{:S(2)}) collective-permute-start(bf16[10,16,256]{2,1,0:T(8,128)(2,1)} %get-tuple-element.1521), channel_id=1, source_target_pairs={{0,8},{4,12},{1,9},{5,13},{2,10},{6,14},{3,11},{7,15},{16,24},{20,... | collective-permute-start | bytes 245768 | tf_op jit(solution)/shard_map/while/body/eval_jaxpr/ppermute | solution.py:14
  206.0 6.5 %select_add_fusion.2 = f32[2,2304,256]{2,1,0:T(8,128)} fusion(f32[2,2304,256]{2,1,0:T(8,128)} %get-tuple-element.1527, f32[2,2304,256]{2,1,0:T(8,128)} %get-tuple-element.1632, pred[]{:T(512)S(6)} %compare.31), kind=kLoop, calls=%fused_computation.218.clone.1 | loop fusion | flops 2359296 | bytes 14155777 | tf_op jit(solution)/shard_map/while/body/eval_jaxpr/add | solution.py:281
  212.5 2.7 collective-permute-done.5
  216.0 3.7 collective-permute-start.8
  225.2 4.5 %conditional.6 = (f32[10,16,256]{2,1,0:T(8,128)}, f32[10,16,256]{2,1,0:T(8,128)}, f32[2,2304,256]{2,1,0:T(8,128)}, bf16[10,16,256]{2,1,0:T(8,128)(2,1)}) conditional(s32[]{:T(128)} %convert_element_type.288, () %tuple.177, (pred[]{:T(512)}, pred[]{:T(512)}, s32[]{:T(128)}, bf16[2,8,16,256]{3,2,1,0:T(8,128)(2,1)}, f32[2,8,16,256]{3,2,1,0:T(8,128)}, ...), branch_computations={%region_7.7_spmd, %region_8.12_spmd} | conditional | flops 608786816 | bytes 39218820 | solution.py:275
  225.2 2.5 broadcast.218
  231.0 13.0 %collective-permute-start.7 = (bf16[10,16,256]{2,1,0:T(8,128)(2,1)}, bf16[10,16,256]{2,1,0:T(8,128)(2,1)}, u32[]{:S(2)}, u32[]{:S(2)}) collective-permute-start(bf16[10,16,256]{2,1,0:T(8,128)(2,1)} %get-tuple-element.1521), channel_id=1, source_target_pairs={{0,8},{4,12},{1,9},{5,13},{2,10},{6,14},{3,11},{7,15},{16,24},{20,... | collective-permute-start | bytes 245768 | tf_op jit(solution)/shard_map/while/body/eval_jaxpr/ppermute | solution.py:14
  246.9 6.5 %select_add_fusion.2 = f32[2,2304,256]{2,1,0:T(8,128)} fusion(f32[2,2304,256]{2,1,0:T(8,128)} %get-tuple-element.1527, f32[2,2304,256]{2,1,0:T(8,128)} %get-tuple-element.1632, pred[]{:T(512)S(6)} %compare.31), kind=kLoop, calls=%fused_computation.218.clone.1 | loop fusion | flops 2359296 | bytes 14155777 | tf_op jit(solution)/shard_map/while/body/eval_jaxpr/add | solution.py:281
  254.2 2.5 collective-permute-start.8
  262.3 9.4 %conditional.6 = (f32[10,16,256]{2,1,0:T(8,128)}, f32[10,16,256]{2,1,0:T(8,128)}, f32[2,2304,256]{2,1,0:T(8,128)}, bf16[10,16,256]{2,1,0:T(8,128)(2,1)}) conditional(s32[]{:T(128)} %convert_element_type.288, () %tuple.177, (pred[]{:T(512)}, pred[]{:T(512)}, s32[]{:T(128)}, bf16[2,8,16,256]{3,2,1,0:T(8,128)(2,1)}, f32[2,8,16,256]{3,2,1,0:T(8,128)}, ...), branch_computations={%region_7.7_spmd, %region_8.12_spmd} | conditional | flops 608786816 | bytes 39218820 | solution.py:275
  268.2 2.5 pad_maximum_fusion.4
  272.9 6.1 %collective-permute-start.7 = (bf16[10,16,256]{2,1,0:T(8,128)(2,1)}, bf16[10,16,256]{2,1,0:T(8,128)(2,1)}, u32[]{:S(2)}, u32[]{:S(2)}) collective-permute-start(bf16[10,16,256]{2,1,0:T(8,128)(2,1)} %get-tuple-element.1521), channel_id=1, source_target_pairs={{0,8},{4,12},{1,9},{5,13},{2,10},{6,14},{3,11},{7,15},{16,24},{20,... | collective-permute-start | bytes 245768 | tf_op jit(solution)/shard_map/while/body/eval_jaxpr/ppermute | solution.py:14
  281.9 6.5 %select_add_fusion.2 = f32[2,2304,256]{2,1,0:T(8,128)} fusion(f32[2,2304,256]{2,1,0:T(8,128)} %get-tuple-element.1527, f32[2,2304,256]{2,1,0:T(8,128)} %get-tuple-element.1632, pred[]{:T(512)S(6)} %compare.31), kind=kLoop, calls=%fused_computation.218.clone.1 | loop fusion | flops 2359296 | bytes 14155777 | tf_op jit(solution)/shard_map/while/body/eval_jaxpr/add | solution.py:281
  289.3 2.8 collective-permute-start.8
  297.6 9.3 %conditional.6 = (f32[10,16,256]{2,1,0:T(8,128)}, f32[10,16,256]{2,1,0:T(8,128)}, f32[2,2304,256]{2,1,0:T(8,128)}, bf16[10,16,256]{2,1,0:T(8,128)(2,1)}) conditional(s32[]{:T(128)} %convert_element_type.288, () %tuple.177, (pred[]{:T(512)}, pred[]{:T(512)}, s32[]{:T(128)}, bf16[2,8,16,256]{3,2,1,0:T(8,128)(2,1)}, f32[2,8,16,256]{3,2,1,0:T(8,128)}, ...), branch_computations={%region_7.7_spmd, %region_8.12_spmd} | conditional | flops 608786816 | bytes 39218820 | solution.py:275
  303.5 2.5 pad_maximum_fusion.4
  308.3 6.1 %collective-permute-start.7 = (bf16[10,16,256]{2,1,0:T(8,128)(2,1)}, bf16[10,16,256]{2,1,0:T(8,128)(2,1)}, u32[]{:S(2)}, u32[]{:S(2)}) collective-permute-start(bf16[10,16,256]{2,1,0:T(8,128)(2,1)} %get-tuple-element.1521), channel_id=1, source_target_pairs={{0,8},{4,12},{1,9},{5,13},{2,10},{6,14},{3,11},{7,15},{16,24},{20,... | collective-permute-start | bytes 245768 | tf_op jit(solution)/shard_map/while/body/eval_jaxpr/ppermute | solution.py:14
  317.3 6.5 %select_add_fusion.2 = f32[2,2304,256]{2,1,0:T(8,128)} fusion(f32[2,2304,256]{2,1,0:T(8,128)} %get-tuple-element.1527, f32[2,2304,256]{2,1,0:T(8,128)} %get-tuple-element.1632, pred[]{:T(512)S(6)} %compare.31), kind=kLoop, calls=%fused_computation.218.clone.1 | loop fusion | flops 2359296 | bytes 14155777 | tf_op jit(solution)/shard_map/while/body/eval_jaxpr/add | solution.py:281
  324.6 2.8 collective-permute-start.8
  331.3 4.0 %convert_element_type.213 = bf16[2,2304,256]{2,1,0:T(8,128)(2,1)} convert(f32[2,2304,256]{2,1,0:T(8,128)} %get-tuple-element.1080) | non-fusion elementwise | flops 1179648 | bytes 7077888 | tf_op jit(solution)/shard_map/convert_element_type | solution.py:292
  335.4 33.9 %reduce-scatter.2.cloned.1.call-done = bf16[2,576,256]{2,1,0:T(8,128)(2,1)} async-done(((bf16[2,2304,256]{2,1,0:T(8,128)(2,1)}), bf16[2,576,256]{2,1,0:T(8,128)(2,1)}) %reduce-scatter.2.cloned.1.call-update) | async-done | bytes 589840 | tf_op jit(solution)/shard_map/reduce_scatter | solution.py:291
  369.3 2.2 bitcast_convert_fusion
  (337 shorter events, 149.3 us)
Async XLA Ops:
  6.5 362.8 %reduce-scatter.2.cloned.1.call-start = ((), (), s32[]{:S(2)}) async-start(), calls=%async_computation.1 | async-start | bytes 2949120 | tf_op jit(solution)/shard_map/reduce_scatter | solution.py:291
  7.4 5.6 %collective-permute-start.10 = (bf16[2,1,16,256]{3,2,1,0:T(8,128)(2,1)S(1)}, bf16[2,1,16,256]{3,2,1,0:T(8,128)(2,1)S(1)}, u32[]{:S(2)}, u32[]{:S(2)}) collective-permute-start(bf16[2,1,16,256]{3,2,1,0:T(8,128)(2,1)S(1)} %get-tuple-element.1274), channel_id=1, source_target_pairs={{0,1},{2,3},{4,5},{6,7},{8,9},{10,11},{12,13},{14,15},{16,17},{18,... | collective-permute-start | bytes 49160 | tf_op jit(solution)/shard_map/ppermute | solution.py:24
  8.9 4.2 %collective-permute-start.11 = (bf16[2,1,16,256]{3,2,1,0:T(8,128)(2,1)S(1)}, bf16[2,1,16,256]{3,2,1,0:T(8,128)(2,1)S(1)}, u32[]{:S(2)}, u32[]{:S(2)}) collective-permute-start(bf16[2,1,16,256]{3,2,1,0:T(8,128)(2,1)S(1)} %get-tuple-element.1275), channel_id=1, source_target_pairs={{1,0},{3,2},{5,4},{7,6},{9,8},{11,10},{13,12},{15,14},{17,16},{19,... | collective-permute-start | bytes 49160 | tf_op jit(solution)/shard_map/ppermute | solution.py:25
  24.6 7.5 %collective-permute-start = (bf16[8,16,256]{2,1,0:T(8,128)(2,1)S(1)}, bf16[8,16,256]{2,1,0:T(8,128)(2,1)S(1)}, u32[]{:S(2)}, u32[]{:S(2)}) collective-permute-start(bf16[8,16,256]{2,1,0:T(8,128)(2,1)S(1)} %get-tuple-element.1492), channel_id=1, source_target_pairs={{0,4},{4,8},{8,12},{1,5},{5,9},{9,13},{2,6},{6,10},{10,14},{3,7},{... | collective-permute-start | bytes 196616 | tf_op jit(solution)/shard_map/while/body/eval_jaxpr/ppermute | solution.py:14
  25.9 7.9 %collective-permute-start.1 = (bf16[8,16,256]{2,1,0:T(8,128)(2,1)S(1)}, bf16[8,16,256]{2,1,0:T(8,128)(2,1)S(1)}, u32[]{:S(2)}, u32[]{:S(2)}) collective-permute-start(bf16[8,16,256]{2,1,0:T(8,128)(2,1)S(1)} %get-tuple-element.1492), channel_id=1, source_target_pairs={{8,0},{12,4},{9,1},{13,5},{10,2},{14,6},{11,3},{15,7},{24,16},{28,... | collective-permute-start | bytes 196616 | tf_op jit(solution)/shard_map/while/body/eval_jaxpr/ppermute | solution.py:14
  27.2 6.6 %collective-permute-start.2 = (bf16[8,16,256]{2,1,0:T(8,128)(2,1)S(1)}, bf16[8,16,256]{2,1,0:T(8,128)(2,1)S(1)}, u32[]{:S(2)}, u32[]{:S(2)}) collective-permute-start(bf16[8,16,256]{2,1,0:T(8,128)(2,1)S(1)} %get-tuple-element.1492), channel_id=1, source_target_pairs={{0,8},{4,12},{1,9},{5,13},{2,10},{6,14},{3,11},{7,15},{16,24},{20,... | collective-permute-start | bytes 196616 | tf_op jit(solution)/shard_map/while/body/eval_jaxpr/ppermute | solution.py:14
  34.6 6.2 %collective-permute-start.3 = (bf16[3,1,16,256]{3,2,1,0:T(8,128)(2,1)}, bf16[3,1,16,256]{3,2,1,0:T(8,128)(2,1)}, u32[]{:S(2)}, u32[]{:S(2)}) collective-permute-start(bf16[3,1,16,256]{3,2,1,0:T(8,128)(2,1)} %get-tuple-element.1493), channel_id=1, source_target_pairs={{1,0},{3,2},{5,4},{7,6},{9,8},{11,10},{13,12},{15,14},{17,16},{19,... | collective-permute-start | bytes 73736 | tf_op jit(solution)/shard_map/while/body/eval_jaxpr/ppermute | solution.py:25
  37.7 3.4 collective-permute-start.4
  49.3 8.2 %collective-permute-start = (bf16[8,16,256]{2,1,0:T(8,128)(2,1)S(1)}, bf16[8,16,256]{2,1,0:T(8,128)(2,1)S(1)}, u32[]{:S(2)}, u32[]{:S(2)}) collective-permute-start(bf16[8,16,256]{2,1,0:T(8,128)(2,1)S(1)} %get-tuple-element.1492), channel_id=1, source_target_pairs={{0,4},{4,8},{8,12},{1,5},{5,9},{9,13},{2,6},{6,10},{10,14},{3,7},{... | collective-permute-start | bytes 196616 | tf_op jit(solution)/shard_map/while/body/eval_jaxpr/ppermute | solution.py:14
  50.6 6.9 %collective-permute-start.1 = (bf16[8,16,256]{2,1,0:T(8,128)(2,1)S(1)}, bf16[8,16,256]{2,1,0:T(8,128)(2,1)S(1)}, u32[]{:S(2)}, u32[]{:S(2)}) collective-permute-start(bf16[8,16,256]{2,1,0:T(8,128)(2,1)S(1)} %get-tuple-element.1492), channel_id=1, source_target_pairs={{8,0},{12,4},{9,1},{13,5},{10,2},{14,6},{11,3},{15,7},{24,16},{28,... | collective-permute-start | bytes 196616 | tf_op jit(solution)/shard_map/while/body/eval_jaxpr/ppermute | solution.py:14
  51.9 6.9 %collective-permute-start.2 = (bf16[8,16,256]{2,1,0:T(8,128)(2,1)S(1)}, bf16[8,16,256]{2,1,0:T(8,128)(2,1)S(1)}, u32[]{:S(2)}, u32[]{:S(2)}) collective-permute-start(bf16[8,16,256]{2,1,0:T(8,128)(2,1)S(1)} %get-tuple-element.1492), channel_id=1, source_target_pairs={{0,8},{4,12},{1,9},{5,13},{2,10},{6,14},{3,11},{7,15},{16,24},{20,... | collective-permute-start | bytes 196616 | tf_op jit(solution)/shard_map/while/body/eval_jaxpr/ppermute | solution.py:14
  59.5 7.7 %collective-permute-start.3 = (bf16[3,1,16,256]{3,2,1,0:T(8,128)(2,1)}, bf16[3,1,16,256]{3,2,1,0:T(8,128)(2,1)}, u32[]{:S(2)}, u32[]{:S(2)}) collective-permute-start(bf16[3,1,16,256]{3,2,1,0:T(8,128)(2,1)} %get-tuple-element.1493), channel_id=1, source_target_pairs={{1,0},{3,2},{5,4},{7,6},{9,8},{11,10},{13,12},{15,14},{17,16},{19,... | collective-permute-start | bytes 73736 | tf_op jit(solution)/shard_map/while/body/eval_jaxpr/ppermute | solution.py:25
  64.2 3.4 collective-permute-start.4
  71.7 16.0 %collective-permute-start = (bf16[8,16,256]{2,1,0:T(8,128)(2,1)S(1)}, bf16[8,16,256]{2,1,0:T(8,128)(2,1)S(1)}, u32[]{:S(2)}, u32[]{:S(2)}) collective-permute-start(bf16[8,16,256]{2,1,0:T(8,128)(2,1)S(1)} %get-tuple-element.1492), channel_id=1, source_target_pairs={{0,4},{4,8},{8,12},{1,5},{5,9},{9,13},{2,6},{6,10},{10,14},{3,7},{... | collective-permute-start | bytes 196616 | tf_op jit(solution)/shard_map/while/body/eval_jaxpr/ppermute | solution.py:14
  77.4 10.3 %collective-permute-start.1 = (bf16[8,16,256]{2,1,0:T(8,128)(2,1)S(1)}, bf16[8,16,256]{2,1,0:T(8,128)(2,1)S(1)}, u32[]{:S(2)}, u32[]{:S(2)}) collective-permute-start(bf16[8,16,256]{2,1,0:T(8,128)(2,1)S(1)} %get-tuple-element.1492), channel_id=1, source_target_pairs={{8,0},{12,4},{9,1},{13,5},{10,2},{14,6},{11,3},{15,7},{24,16},{28,... | collective-permute-start | bytes 196616 | tf_op jit(solution)/shard_map/while/body/eval_jaxpr/ppermute | solution.py:14
  78.7 10.3 %collective-permute-start.2 = (bf16[8,16,256]{2,1,0:T(8,128)(2,1)S(1)}, bf16[8,16,256]{2,1,0:T(8,128)(2,1)S(1)}, u32[]{:S(2)}, u32[]{:S(2)}) collective-permute-start(bf16[8,16,256]{2,1,0:T(8,128)(2,1)S(1)} %get-tuple-element.1492), channel_id=1, source_target_pairs={{0,8},{4,12},{1,9},{5,13},{2,10},{6,14},{3,11},{7,15},{16,24},{20,... | collective-permute-start | bytes 196616 | tf_op jit(solution)/shard_map/while/body/eval_jaxpr/ppermute | solution.py:14
  89.7 8.0 %collective-permute-start.3 = (bf16[3,1,16,256]{3,2,1,0:T(8,128)(2,1)}, bf16[3,1,16,256]{3,2,1,0:T(8,128)(2,1)}, u32[]{:S(2)}, u32[]{:S(2)}) collective-permute-start(bf16[3,1,16,256]{3,2,1,0:T(8,128)(2,1)} %get-tuple-element.1493), channel_id=1, source_target_pairs={{1,0},{3,2},{5,4},{7,6},{9,8},{11,10},{13,12},{15,14},{17,16},{19,... | collective-permute-start | bytes 73736 | tf_op jit(solution)/shard_map/while/body/eval_jaxpr/ppermute | solution.py:25
  94.6 3.4 collective-permute-start.4
  102.1 12.0 %collective-permute-start = (bf16[8,16,256]{2,1,0:T(8,128)(2,1)S(1)}, bf16[8,16,256]{2,1,0:T(8,128)(2,1)S(1)}, u32[]{:S(2)}, u32[]{:S(2)}) collective-permute-start(bf16[8,16,256]{2,1,0:T(8,128)(2,1)S(1)} %get-tuple-element.1492), channel_id=1, source_target_pairs={{0,4},{4,8},{8,12},{1,5},{5,9},{9,13},{2,6},{6,10},{10,14},{3,7},{... | collective-permute-start | bytes 196616 | tf_op jit(solution)/shard_map/while/body/eval_jaxpr/ppermute | solution.py:14
  107.9 6.3 %collective-permute-start.1 = (bf16[8,16,256]{2,1,0:T(8,128)(2,1)S(1)}, bf16[8,16,256]{2,1,0:T(8,128)(2,1)S(1)}, u32[]{:S(2)}, u32[]{:S(2)}) collective-permute-start(bf16[8,16,256]{2,1,0:T(8,128)(2,1)S(1)} %get-tuple-element.1492), channel_id=1, source_target_pairs={{8,0},{12,4},{9,1},{13,5},{10,2},{14,6},{11,3},{15,7},{24,16},{28,... | collective-permute-start | bytes 196616 | tf_op jit(solution)/shard_map/while/body/eval_jaxpr/ppermute | solution.py:14
  109.2 6.3 %collective-permute-start.2 = (bf16[8,16,256]{2,1,0:T(8,128)(2,1)S(1)}, bf16[8,16,256]{2,1,0:T(8,128)(2,1)S(1)}, u32[]{:S(2)}, u32[]{:S(2)}) collective-permute-start(bf16[8,16,256]{2,1,0:T(8,128)(2,1)S(1)} %get-tuple-element.1492), channel_id=1, source_target_pairs={{0,8},{4,12},{1,9},{5,13},{2,10},{6,14},{3,11},{7,15},{16,24},{20,... | collective-permute-start | bytes 196616 | tf_op jit(solution)/shard_map/while/body/eval_jaxpr/ppermute | solution.py:14
  116.1 8.2 %collective-permute-start.3 = (bf16[3,1,16,256]{3,2,1,0:T(8,128)(2,1)}, bf16[3,1,16,256]{3,2,1,0:T(8,128)(2,1)}, u32[]{:S(2)}, u32[]{:S(2)}) collective-permute-start(bf16[3,1,16,256]{3,2,1,0:T(8,128)(2,1)} %get-tuple-element.1493), channel_id=1, source_target_pairs={{1,0},{3,2},{5,4},{7,6},{9,8},{11,10},{13,12},{15,14},{17,16},{19,... | collective-permute-start | bytes 73736 | tf_op jit(solution)/shard_map/while/body/eval_jaxpr/ppermute | solution.py:25
  121.3 3.4 collective-permute-start.4
  128.8 11.9 %collective-permute-start = (bf16[8,16,256]{2,1,0:T(8,128)(2,1)S(1)}, bf16[8,16,256]{2,1,0:T(8,128)(2,1)S(1)}, u32[]{:S(2)}, u32[]{:S(2)}) collective-permute-start(bf16[8,16,256]{2,1,0:T(8,128)(2,1)S(1)} %get-tuple-element.1492), channel_id=1, source_target_pairs={{0,4},{4,8},{8,12},{1,5},{5,9},{9,13},{2,6},{6,10},{10,14},{3,7},{... | collective-permute-start | bytes 196616 | tf_op jit(solution)/shard_map/while/body/eval_jaxpr/ppermute | solution.py:14
  134.6 6.3 %collective-permute-start.1 = (bf16[8,16,256]{2,1,0:T(8,128)(2,1)S(1)}, bf16[8,16,256]{2,1,0:T(8,128)(2,1)S(1)}, u32[]{:S(2)}, u32[]{:S(2)}) collective-permute-start(bf16[8,16,256]{2,1,0:T(8,128)(2,1)S(1)} %get-tuple-element.1492), channel_id=1, source_target_pairs={{8,0},{12,4},{9,1},{13,5},{10,2},{14,6},{11,3},{15,7},{24,16},{28,... | collective-permute-start | bytes 196616 | tf_op jit(solution)/shard_map/while/body/eval_jaxpr/ppermute | solution.py:14
  135.9 6.2 %collective-permute-start.2 = (bf16[8,16,256]{2,1,0:T(8,128)(2,1)S(1)}, bf16[8,16,256]{2,1,0:T(8,128)(2,1)S(1)}, u32[]{:S(2)}, u32[]{:S(2)}) collective-permute-start(bf16[8,16,256]{2,1,0:T(8,128)(2,1)S(1)} %get-tuple-element.1492), channel_id=1, source_target_pairs={{0,8},{4,12},{1,9},{5,13},{2,10},{6,14},{3,11},{7,15},{16,24},{20,... | collective-permute-start | bytes 196616 | tf_op jit(solution)/shard_map/while/body/eval_jaxpr/ppermute | solution.py:14
  142.7 8.3 %collective-permute-start.3 = (bf16[3,1,16,256]{3,2,1,0:T(8,128)(2,1)}, bf16[3,1,16,256]{3,2,1,0:T(8,128)(2,1)}, u32[]{:S(2)}, u32[]{:S(2)}) collective-permute-start(bf16[3,1,16,256]{3,2,1,0:T(8,128)(2,1)} %get-tuple-element.1493), channel_id=1, source_target_pairs={{1,0},{3,2},{5,4},{7,6},{9,8},{11,10},{13,12},{15,14},{17,16},{19,... | collective-permute-start | bytes 73736 | tf_op jit(solution)/shard_map/while/body/eval_jaxpr/ppermute | solution.py:25
  148.0 3.4 collective-permute-start.4
  161.9 17.7 %collective-permute-start.6 = (bf16[10,16,256]{2,1,0:T(8,128)(2,1)}, bf16[10,16,256]{2,1,0:T(8,128)(2,1)}, u32[]{:S(2)}, u32[]{:S(2)}) collective-permute-start(bf16[10,16,256]{2,1,0:T(8,128)(2,1)} %get-tuple-element.1521), channel_id=1, source_target_pairs={{8,0},{12,4},{9,1},{13,5},{10,2},{14,6},{11,3},{15,7},{24,16},{28,... | collective-permute-start | bytes 245768 | tf_op jit(solution)/shard_map/while/body/eval_jaxpr/ppermute | solution.py:14
  163.2 16.4 %collective-permute-start.7 = (bf16[10,16,256]{2,1,0:T(8,128)(2,1)}, bf16[10,16,256]{2,1,0:T(8,128)(2,1)}, u32[]{:S(2)}, u32[]{:S(2)}) collective-permute-start(bf16[10,16,256]{2,1,0:T(8,128)(2,1)} %get-tuple-element.1521), channel_id=1, source_target_pairs={{0,8},{4,12},{1,9},{5,13},{2,10},{6,14},{3,11},{7,15},{16,24},{20,... | collective-permute-start | bytes 245768 | tf_op jit(solution)/shard_map/while/body/eval_jaxpr/ppermute | solution.py:14
  170.9 8.7 %collective-permute-start.5 = (bf16[10,16,256]{2,1,0:T(8,128)(2,1)}, bf16[10,16,256]{2,1,0:T(8,128)(2,1)}, u32[]{:S(2)}, u32[]{:S(2)}) collective-permute-start(bf16[10,16,256]{2,1,0:T(8,128)(2,1)} %add_convert_fusion.2), channel_id=1, source_target_pairs={{4,0},{8,4},{12,8},{5,1},{9,5},{13,9},{6,2},{10,6},{14,10},{7,3},{... | collective-permute-start | bytes 245768 | tf_op jit(solution)/shard_map/while/body/eval_jaxpr/ppermute | solution.py:14
  180.4 7.0 %collective-permute-start.8 = (bf16[3,1,16,256]{3,2,1,0:T(8,128)(2,1)S(1)}, bf16[3,1,16,256]{3,2,1,0:T(8,128)(2,1)S(1)}, u32[]{:S(2)}, u32[]{:S(2)}) collective-permute-start(bf16[3,1,16,256]{3,2,1,0:T(8,128)(2,1)S(1)} %get-tuple-element.1522), channel_id=1, source_target_pairs={{1,0},{3,2},{5,4},{7,6},{9,8},{11,10},{13,12},{15,14},{17,16},{19,... | collective-permute-start | bytes 73736 | tf_op jit(solution)/shard_map/while/body/eval_jaxpr/ppermute | solution.py:25
  195.1 20.1 %collective-permute-start.6 = (bf16[10,16,256]{2,1,0:T(8,128)(2,1)}, bf16[10,16,256]{2,1,0:T(8,128)(2,1)}, u32[]{:S(2)}, u32[]{:S(2)}) collective-permute-start(bf16[10,16,256]{2,1,0:T(8,128)(2,1)} %get-tuple-element.1521), channel_id=1, source_target_pairs={{8,0},{12,4},{9,1},{13,5},{10,2},{14,6},{11,3},{15,7},{24,16},{28,... | collective-permute-start | bytes 245768 | tf_op jit(solution)/shard_map/while/body/eval_jaxpr/ppermute | solution.py:14
  196.4 18.8 %collective-permute-start.7 = (bf16[10,16,256]{2,1,0:T(8,128)(2,1)}, bf16[10,16,256]{2,1,0:T(8,128)(2,1)}, u32[]{:S(2)}, u32[]{:S(2)}) collective-permute-start(bf16[10,16,256]{2,1,0:T(8,128)(2,1)} %get-tuple-element.1521), channel_id=1, source_target_pairs={{0,8},{4,12},{1,9},{5,13},{2,10},{6,14},{3,11},{7,15},{16,24},{20,... | collective-permute-start | bytes 245768 | tf_op jit(solution)/shard_map/while/body/eval_jaxpr/ppermute | solution.py:14
  204.7 10.5 %collective-permute-start.5 = (bf16[10,16,256]{2,1,0:T(8,128)(2,1)}, bf16[10,16,256]{2,1,0:T(8,128)(2,1)}, u32[]{:S(2)}, u32[]{:S(2)}) collective-permute-start(bf16[10,16,256]{2,1,0:T(8,128)(2,1)} %add_convert_fusion.2), channel_id=1, source_target_pairs={{4,0},{8,4},{12,8},{5,1},{9,5},{13,9},{6,2},{10,6},{14,10},{7,3},{... | collective-permute-start | bytes 245768 | tf_op jit(solution)/shard_map/while/body/eval_jaxpr/ppermute | solution.py:14
  216.0 6.0 %collective-permute-start.8 = (bf16[3,1,16,256]{3,2,1,0:T(8,128)(2,1)S(1)}, bf16[3,1,16,256]{3,2,1,0:T(8,128)(2,1)S(1)}, u32[]{:S(2)}, u32[]{:S(2)}) collective-permute-start(bf16[3,1,16,256]{3,2,1,0:T(8,128)(2,1)S(1)} %get-tuple-element.1522), channel_id=1, source_target_pairs={{1,0},{3,2},{5,4},{7,6},{9,8},{11,10},{13,12},{15,14},{17,16},{19,... | collective-permute-start | bytes 73736 | tf_op jit(solution)/shard_map/while/body/eval_jaxpr/ppermute | solution.py:25
  229.7 23.7 %collective-permute-start.6 = (bf16[10,16,256]{2,1,0:T(8,128)(2,1)}, bf16[10,16,256]{2,1,0:T(8,128)(2,1)}, u32[]{:S(2)}, u32[]{:S(2)}) collective-permute-start(bf16[10,16,256]{2,1,0:T(8,128)(2,1)} %get-tuple-element.1521), channel_id=1, source_target_pairs={{8,0},{12,4},{9,1},{13,5},{10,2},{14,6},{11,3},{15,7},{24,16},{28,... | collective-permute-start | bytes 245768 | tf_op jit(solution)/shard_map/while/body/eval_jaxpr/ppermute | solution.py:14
  231.0 22.4 %collective-permute-start.7 = (bf16[10,16,256]{2,1,0:T(8,128)(2,1)}, bf16[10,16,256]{2,1,0:T(8,128)(2,1)}, u32[]{:S(2)}, u32[]{:S(2)}) collective-permute-start(bf16[10,16,256]{2,1,0:T(8,128)(2,1)} %get-tuple-element.1521), channel_id=1, source_target_pairs={{0,8},{4,12},{1,9},{5,13},{2,10},{6,14},{3,11},{7,15},{16,24},{20,... | collective-permute-start | bytes 245768 | tf_op jit(solution)/shard_map/while/body/eval_jaxpr/ppermute | solution.py:14
  245.6 7.8 %collective-permute-start.5 = (bf16[10,16,256]{2,1,0:T(8,128)(2,1)}, bf16[10,16,256]{2,1,0:T(8,128)(2,1)}, u32[]{:S(2)}, u32[]{:S(2)}) collective-permute-start(bf16[10,16,256]{2,1,0:T(8,128)(2,1)} %add_convert_fusion.2), channel_id=1, source_target_pairs={{4,0},{8,4},{12,8},{5,1},{9,5},{13,9},{6,2},{10,6},{14,10},{7,3},{... | collective-permute-start | bytes 245768 | tf_op jit(solution)/shard_map/while/body/eval_jaxpr/ppermute | solution.py:14
  254.2 4.9 %collective-permute-start.8 = (bf16[3,1,16,256]{3,2,1,0:T(8,128)(2,1)S(1)}, bf16[3,1,16,256]{3,2,1,0:T(8,128)(2,1)S(1)}, u32[]{:S(2)}, u32[]{:S(2)}) collective-permute-start(bf16[3,1,16,256]{3,2,1,0:T(8,128)(2,1)S(1)} %get-tuple-element.1522), channel_id=1, source_target_pairs={{1,0},{3,2},{5,4},{7,6},{9,8},{11,10},{13,12},{15,14},{17,16},{19,... | collective-permute-start | bytes 73736 | tf_op jit(solution)/shard_map/while/body/eval_jaxpr/ppermute | solution.py:25
  271.6 16.8 %collective-permute-start.6 = (bf16[10,16,256]{2,1,0:T(8,128)(2,1)}, bf16[10,16,256]{2,1,0:T(8,128)(2,1)}, u32[]{:S(2)}, u32[]{:S(2)}) collective-permute-start(bf16[10,16,256]{2,1,0:T(8,128)(2,1)} %get-tuple-element.1521), channel_id=1, source_target_pairs={{8,0},{12,4},{9,1},{13,5},{10,2},{14,6},{11,3},{15,7},{24,16},{28,... | collective-permute-start | bytes 245768 | tf_op jit(solution)/shard_map/while/body/eval_jaxpr/ppermute | solution.py:14
  272.9 15.5 %collective-permute-start.7 = (bf16[10,16,256]{2,1,0:T(8,128)(2,1)}, bf16[10,16,256]{2,1,0:T(8,128)(2,1)}, u32[]{:S(2)}, u32[]{:S(2)}) collective-permute-start(bf16[10,16,256]{2,1,0:T(8,128)(2,1)} %get-tuple-element.1521), channel_id=1, source_target_pairs={{0,8},{4,12},{1,9},{5,13},{2,10},{6,14},{3,11},{7,15},{16,24},{20,... | collective-permute-start | bytes 245768 | tf_op jit(solution)/shard_map/while/body/eval_jaxpr/ppermute | solution.py:14
  280.6 7.8 %collective-permute-start.5 = (bf16[10,16,256]{2,1,0:T(8,128)(2,1)}, bf16[10,16,256]{2,1,0:T(8,128)(2,1)}, u32[]{:S(2)}, u32[]{:S(2)}) collective-permute-start(bf16[10,16,256]{2,1,0:T(8,128)(2,1)} %add_convert_fusion.2), channel_id=1, source_target_pairs={{4,0},{8,4},{12,8},{5,1},{9,5},{13,9},{6,2},{10,6},{14,10},{7,3},{... | collective-permute-start | bytes 245768 | tf_op jit(solution)/shard_map/while/body/eval_jaxpr/ppermute | solution.py:14
  289.3 5.1 %collective-permute-start.8 = (bf16[3,1,16,256]{3,2,1,0:T(8,128)(2,1)S(1)}, bf16[3,1,16,256]{3,2,1,0:T(8,128)(2,1)S(1)}, u32[]{:S(2)}, u32[]{:S(2)}) collective-permute-start(bf16[3,1,16,256]{3,2,1,0:T(8,128)(2,1)S(1)} %get-tuple-element.1522), channel_id=1, source_target_pairs={{1,0},{3,2},{5,4},{7,6},{9,8},{11,10},{13,12},{15,14},{17,16},{19,... | collective-permute-start | bytes 73736 | tf_op jit(solution)/shard_map/while/body/eval_jaxpr/ppermute | solution.py:25
  307.0 16.8 %collective-permute-start.6 = (bf16[10,16,256]{2,1,0:T(8,128)(2,1)}, bf16[10,16,256]{2,1,0:T(8,128)(2,1)}, u32[]{:S(2)}, u32[]{:S(2)}) collective-permute-start(bf16[10,16,256]{2,1,0:T(8,128)(2,1)} %get-tuple-element.1521), channel_id=1, source_target_pairs={{8,0},{12,4},{9,1},{13,5},{10,2},{14,6},{11,3},{15,7},{24,16},{28,... | collective-permute-start | bytes 245768 | tf_op jit(solution)/shard_map/while/body/eval_jaxpr/ppermute | solution.py:14
  308.3 15.5 %collective-permute-start.7 = (bf16[10,16,256]{2,1,0:T(8,128)(2,1)}, bf16[10,16,256]{2,1,0:T(8,128)(2,1)}, u32[]{:S(2)}, u32[]{:S(2)}) collective-permute-start(bf16[10,16,256]{2,1,0:T(8,128)(2,1)} %get-tuple-element.1521), channel_id=1, source_target_pairs={{0,8},{4,12},{1,9},{5,13},{2,10},{6,14},{3,11},{7,15},{16,24},{20,... | collective-permute-start | bytes 245768 | tf_op jit(solution)/shard_map/while/body/eval_jaxpr/ppermute | solution.py:14
  316.0 7.8 %collective-permute-start.5 = (bf16[10,16,256]{2,1,0:T(8,128)(2,1)}, bf16[10,16,256]{2,1,0:T(8,128)(2,1)}, u32[]{:S(2)}, u32[]{:S(2)}) collective-permute-start(bf16[10,16,256]{2,1,0:T(8,128)(2,1)} %add_convert_fusion.2), channel_id=1, source_target_pairs={{4,0},{8,4},{12,8},{5,1},{9,5},{13,9},{6,2},{10,6},{14,10},{7,3},{... | collective-permute-start | bytes 245768 | tf_op jit(solution)/shard_map/while/body/eval_jaxpr/ppermute | solution.py:14
  324.6 5.1 %collective-permute-start.8 = (bf16[3,1,16,256]{3,2,1,0:T(8,128)(2,1)S(1)}, bf16[3,1,16,256]{3,2,1,0:T(8,128)(2,1)S(1)}, u32[]{:S(2)}, u32[]{:S(2)}) collective-permute-start(bf16[3,1,16,256]{3,2,1,0:T(8,128)(2,1)S(1)} %get-tuple-element.1522), channel_id=1, source_target_pairs={{1,0},{3,2},{5,4},{7,6},{9,8},{11,10},{13,12},{15,14},{17,16},{19,... | collective-permute-start | bytes 73736 | tf_op jit(solution)/shard_map/while/body/eval_jaxpr/ppermute | solution.py:25
  (25 other events, 64.3 us)
Sparse Core Ops, SparseCore 0:
  335.5 33.7 reduce-scatter.1
where the time goes:
time: 382 us; the launch traced here: 378 us
  starting transfers between devices  163 us (43%)
  other arithmetic  106 us (28%)
  waiting for transfers between devices  51.7 us (14%)
  local copies, waits for them, and re-layouts  32.1 us (8%)
  between operations  13.4 us (4%)
  matrix products  9.72 us (3%)
    ppermute x30, starting transfers between devices, passed_along(): lax.ppermute(value, axis, [(source, source + steps) for source in range(l...  106 us
    ppermute x11, starting transfers between devices, padded_2(): after = lax.ppermute(leading, axis, down)  42.8 us
    reduce_scatter x1, waiting for transfers between devices, shards(): lax.psum_scatter(weight_terms.astype(jnp.bfloat16), ('dp', 'space'), scat...  33.9 us
    add x5, other arithmetic, backward_tick(): weight_terms = weight_terms + step_terms  31.2 us
    another operation x18, local copies, waits for them, and re-layouts  15.5 us
    ppermute x11, starting transfers between devices, padded_2(): before = lax.ppermute(last, axis, up)  14.3 us
    ppermute x30, waiting for transfers between devices, passed_along(): lax.ppermute(value, axis, [(source, source + steps) for source in range(l...  11.8 us
    select_n x5, other arithmetic, forward_tick(): jnp.where(active, lax.dynamic_update_index_in_dim(pq_store, jnp.stack([p_...  8.71 us
  transfers between devices with their start and end apart: 53, of which 20 were waited for; matrix products, arithmetic and copies ran while one was open for 14% of the time, Pallas kernels for 0%

commit v1 on v0

v1 whole, which is shorter than its diff:
```python
import functools
import math

import jax
import jax.numpy as jnp
from jax import lax
from jax.experimental import pallas as pl
from jax.experimental.pallas import tpu as pltpu
from jax.sharding import PartitionSpec as P

EPSILON = 1e-06
MESH = pl.DeviceIdType.MESH
X, SKIP, G, GSKIP = range(4)


def sigmoid(z):
    return 0.5 + 0.5 * jnp.tanh(0.5 * z)


def inv_rms(x):
    return lax.rsqrt(jnp.mean(x * x, axis=-1, keepdims=True) + EPSILON)


def normalize(x, gain):
    z = x * inv_rms(x) * gain
    return z * sigmoid(z)


def pull_back(x, gain, grad_f):
    r = inv_rms(x)
    xr = x * r
    z = xr * gain
    s = sigmoid(z)
    u = grad_f * (s * (1.0 + z * (1.0 - s))) * gain
    return r * (u - xr * jnp.mean(xr * u, axis=-1, keepdims=True))


def store_shifts(value, cols, ref, start):
    n = value.shape[0]
    col = lax.broadcasted_iota(jnp.int32, value.shape, 0) % cols
    before = jnp.where(col == 0, 0.0, pltpu.roll(value, 1, 0))
    after = jnp.where(col == cols - 1, 0.0, pltpu.roll(value, n - 1, 0))
    ref[0, start : start + n, :] = before.astype(jnp.bfloat16)
    ref[1, start : start + n, :] = value.astype(jnp.bfloat16)
    ref[2, start : start + n, :] = after.astype(jnp.bfloat16)


def kernel(
    sections, replicas, micro, rows, cols, ch, taps, own_taps, loss_scale,
    ts_ref, images, table, weight, gains, out_grad, result,
    framed, pq, yout, sout, grad_f, shift, w, wt, tab, gn, gain_mod,
    f_all, g_all, ft, gshift, acc,
    lsem, band_s, band_r, halo_s, halo_r, pq_s, pq_r, f_s, f_r, g_s, g_r,
):
    sec = lax.axis_index("section")
    d = lax.axis_index("dp")
    h = lax.axis_index("space")
    other = 1 - h
    block = sec // 2
    enc = sec % 2 == 0
    dec = jnp.logical_not(enc)
    first, last = sec == 0, sec == 1
    turn = block == sections // 2 - 1
    follow = jnp.where(enc, jnp.where(turn, sec + 1, sec + 2), jnp.where(last, 0, sec - 2))
    ahead = jnp.where(dec, jnp.where(turn, sec - 1, sec + 2), jnp.where(first, 1, sec - 2))
    pair = jnp.where(enc, sec + 1, sec - 1)
    use_skip = jnp.logical_and(dec, jnp.logical_not(turn))
    use_gskip = jnp.logical_and(enc, jnp.logical_not(turn))
    pixels = rows * cols
    frame = pixels + 2 * cols
    peers = replicas * 2
    me = d * 2 + h
    band = pl.ds(cols, pixels)
    halo_out = pl.multiple_of(h * (pixels + cols), cols)
    halo_in = pl.multiple_of(other * (pixels + cols), cols)
    edge = pl.multiple_of(other * (pixels - cols), cols)

    def local(src, dst, i):
        return pltpu.make_async_copy(src, dst, lsem.at[i])

    def image_copy(m):
        return local(images.at[m], framed.at[X, m, band], m)

    def seed_copy(m):
        return local(out_grad.at[m], framed.at[G, m, band], micro + m)

    table_copy = local(table, tab, 2 * micro)
    gains_copy = local(gains, gn, 2 * micro + 1)
    weight_copy = local(weight, w, 2 * micro + 2)
    for m in range(micro):
        pl.when(first)(lambda m=m: image_copy(m).start())
        pl.when(last)(lambda m=m: seed_copy(m).start())
    table_copy.start()
    gains_copy.start()
    weight_copy.start()

    barrier = pltpu.get_barrier_semaphore()
    for s in (follow, ahead, pair):
        for side in range(2):
            pl.semaphore_signal(
                barrier, inc=1, device_id={"section": s, "space": side}, device_id_type=MESH
            )
    for k in range(1, peers):
        to = lax.rem(me + k, peers)
        pl.semaphore_signal(
            barrier, inc=1, device_id={"dp": to // 2, "space": to % 2}, device_id_type=MESH
        )

    zero_row = jnp.zeros((cols, ch), jnp.bfloat16)
    for m in range(micro):
        for kind in range(4):
            framed[kind, m, pl.ds(halo_out, cols), :] = zero_row
        for br in range(2):
            pq[m, br, pl.ds(halo_out, cols), :] = jnp.zeros((cols, ch), jnp.float32)
    for br in range(2):
        for k in range(3):
            gshift[br, k, 0:cols, :] = zero_row
            gshift[br, k, cols + 2 * pixels : 2 * cols + 2 * pixels, :] = zero_row
    acc[...] = jnp.zeros_like(acc)
    pl.semaphore_wait(barrier, 6 + peers - 1)

    def band_copy(kind, m, src, to):
        return pltpu.make_async_remote_copy(
            src, framed.at[kind, m, band], band_s.at[kind, m], band_r.at[kind, m],
            device_id={"section": to}, device_id_type=MESH,
        )

    def halo_copy(kind, m, src, to):
        return pltpu.make_async_remote_copy(
            src, framed.at[kind, m, pl.ds(halo_out, cols)],
            halo_s.at[kind, m], halo_r.at[kind, m],
            device_id={"section": to, "space": other}, device_id_type=MESH,
        )

    def sends(kind, m, src, to):
        return (
            halo_copy(kind, m, src.at[m, pl.ds(edge, cols)], to),
            band_copy(kind, m, src.at[m], to),
        )

    def rim_send(kind, m):
        src = framed.at[kind, m, pl.ds(pl.multiple_of(edge + cols, cols), cols)]
        return halo_copy(kind, m, src, sec)

    def band_wait(kind, m):
        band_copy(kind, m, yout.at[m], sec).wait_recv()

    def halo_wait(kind, m):
        pltpu.make_async_remote_copy(
            yout.at[m, pl.ds(0, cols)], framed.at[kind, m, pl.ds(halo_in, cols)],
            halo_s.at[kind, m], halo_r.at[kind, m],
            device_id={"section": sec, "space": other}, device_id_type=MESH,
        ).wait_recv()

    def pq_copy(m):
        return pltpu.make_async_remote_copy(
            pq.at[m, :, pl.ds(pl.multiple_of(edge + cols, cols), cols)],
            pq.at[m, :, pl.ds(halo_out, cols)],
            pq_s.at[m], pq_r.at[m], device_id={"space": other}, device_id_type=MESH,
        )

    def pq_wait(m):
        pltpu.make_async_remote_copy(
            pq.at[m, :, pl.ds(cols, cols)], pq.at[m, :, pl.ds(halo_in, cols)],
            pq_s.at[m], pq_r.at[m], device_id={"space": other}, device_id_type=MESH,
        ).wait_recv()

    def share(ref, send, recv, m, k):
        to = lax.rem(me + k, peers)
        return pltpu.make_async_remote_copy(
            ref.at[d * micro + m, h], ref.at[d * micro + m, h], send.at[k, m], recv.at[k, m],
            device_id={"dp": to // 2, "space": to % 2}, device_id_type=MESH,
        )

    def share_wait(ref, send, recv, m, k):
        source = lax.rem(me - k + peers, peers)
        slot = ref.at[source // 2 * micro + m, source % 2]
        pltpu.make_async_remote_copy(
            slot, slot, send.at[k, m], recv.at[k, m],
            device_id={"dp": source // 2, "space": source % 2}, device_id_type=MESH,
        ).wait_recv()

    def each_micro(body):
        lax.fori_loop(0, micro, lambda m, c: (body(m), c)[1], 0)

    def start_rims():
        def images_in(m):
            image_copy(m).wait()
            rim_send(X, m).start()

        def seeds_in(m):
            seed_copy(m).wait()
            rim_send(G, m).start()

        pl.when(first)(lambda: each_micro(images_in))
        pl.when(last)(lambda: each_micro(seeds_in))

    start_rims()
    table_copy.wait()
    gains_copy.wait()
    for m in range(micro):
        modulation = 1.0 + tab[pl.ds(ts_ref[m], 1), :]
        gain_mod[m, :, :] = gn[...] * modulation
    weight_copy.wait()

    def gain_of(m, br):
        return gain_mod[m, pl.ds(br, 1), :]

    def wait_inputs(m):
        pl.when(jnp.logical_not(first))(lambda: band_wait(X, m))
        halo_wait(X, m)

        @pl.when(use_skip)
        def _():
            band_wait(SKIP, m)
            halo_wait(SKIP, m)

    def inputs(m, part):
        a = framed[X, m, part, :].astype(jnp.float32)
        v = jnp.where(use_skip, framed[SKIP, m, part, :].astype(jnp.float32), a)
        return a, v

    def share_f(m):
        for k in range(1, peers):
            share(f_all, f_s, f_r, m, k).start()

    def share_g(m):
        for k in range(1, peers):
            share(g_all, g_s, g_r, m, k).start()

    def conv(kernels, br, backward):
        pieces = []
        for t in range(9):
            i, j = t // 3, t % 3
            if backward:
                i, j = 2 - i, 2 - j
            pieces.append(shift[br, j, i * cols : i * cols + pixels, :])
        lhs = jnp.concatenate(pieces, axis=1)
        return jnp.dot(lhs, kernels[br], preferred_element_type=jnp.float32)

    def forward(m):
        wait_inputs(m)
        a, v = inputs(m, pl.ds(0, frame))
        for br, x in ((0, a), (1, v)):
            f = normalize(x, gain_of(m, br))
            store_shifts(f, cols, shift.at[br], 0)
            f_all[d * micro + m, h, br, :, :] = shift[br, 1, cols : cols + pixels, :]
        p = conv(w, 0, False)
        q = conv(w, 1, False)
        centre = framed[X, m, band, :].astype(jnp.float32)
        y = jnp.where(enc, centre + p * sigmoid(q), centre + p + q)
        yout[m] = y.astype(jnp.bfloat16)
        for copy in sends(X, m, yout, follow):
            copy.start()

        @pl.when(use_gskip)
        def _():
            for copy in sends(SKIP, m, yout, pair):
                copy.start()

        pq[m, 0, band, :] = p
        pq[m, 1, band, :] = q
        pq_copy(m).start()
        share_f(m)

    def transposes():
        def one(t, c):
            at = pl.ds(pl.multiple_of(t * ch, ch), ch)
            for br in range(2):
                wt[br, at, :] = w[br, at, :].T
            return c

        lax.fori_loop(0, 9, one, 0)

    def field_grads(m):
        pl.when(jnp.logical_not(last))(lambda: band_wait(G, m))
        halo_wait(G, m)

        @pl.when(use_gskip)
        def _():
            band_wait(GSKIP, m)
            halo_wait(GSKIP, m)

        g = out_gradient(m, pl.ds(0, frame))
        s = sigmoid(pq[m, 1])
        gp = jnp.where(enc, g * s, g)
        gq = jnp.where(enc, g * pq[m, 0] * s * (1.0 - s), g)
        for br, grad in ((0, gp), (1, gq)):
            store_shifts(grad, cols, shift.at[br], 0)
            g_all[d * micro + m, h, br, :, :] = shift[br, 1, cols : cols + pixels, :]
        pl.when(first)(lambda: share_g(m))

        @pl.when(jnp.logical_not(first))
        def _():
            for br in range(2):
                grad_f[m, br] = conv(wt, br, True)

    def out_gradient(m, part):
        g = framed[G, m, part, :].astype(jnp.float32)
        g = g + jnp.where(use_gskip, framed[GSKIP, m, part, :].astype(jnp.float32), 0.0)
        return g * jnp.where(last, loss_scale, 1.0)

    def pass_grads(m):
        a, v = inputs(m, band)
        main = pull_back(a, gain_of(m, 0), grad_f[m, 0])
        side = pull_back(v, gain_of(m, 1), grad_f[m, 1])
        g = out_gradient(m, band)
        yout_g = g + main + jnp.where(use_skip, 0.0, side)
        sout[0, m] = yout_g.astype(jnp.bfloat16)
        for copy in sends(G, m, sout.at[0], ahead):
            copy.start()

        @pl.when(use_skip)
        def _():
            sout[1, m] = side.astype(jnp.bfloat16)
            for copy in sends(GSKIP, m, sout.at[1], pair):
                copy.start()

        share_g(m)

    def late_fields(m):
        a, v = inputs(m, band)
        for br, x in ((0, a), (1, v)):
            f_all[d * micro + m, h, br, :, :] = normalize(x, gain_of(m, br)).astype(jnp.bfloat16)
        share_f(m)

    def gather_fields():
        def one(m):
            for k in range(1, peers):
                share_wait(f_all, f_s, f_r, m, k)

            def flip(r, c):
                for br in range(2):
                    for side in range(2):
                        at = slice(side * pixels, (side + 1) * pixels)
                        ft[r * micro + m, br, :, at] = f_all[r * micro + m, side, br].T
                return c

            lax.fori_loop(0, replicas, flip, 0)

        each_micro(one)

    def last_section():
        transposes()
        each_micro(field_grads)

        def one(m):
            wait_inputs(m)
            pass_grads(m)

        each_micro(one)
        each_micro(late_fields)
        gather_fields()

    def other_sections():
        each_micro(forward)
        pl.when(jnp.logical_not(first))(transposes)
        each_micro(pq_wait)
        pl.when(enc)(gather_fields)

        def one(m):
            field_grads(m)
            pl.when(jnp.logical_not(first))(lambda: pass_grads(m))

        each_micro(one)
        pl.when(dec)(gather_fields)

    pl.when(last)(last_section)
    pl.when(jnp.logical_not(last))(other_sections)

    own = 9 * ch // peers
    tap0 = jnp.minimum(me * own // ch, 9 - own_taps)
    offset = pl.multiple_of(me * own - tap0 * ch, 16)

    def weight_terms(m):
        for k in range(1, peers):
            share_wait(g_all, g_s, g_r, m, k)

        def one(r, c):
            image = r * micro + m
            for br in range(2):
                for side in range(2):
                    store_shifts(
                        g_all[image, side, br].astype(jnp.float32),
                        cols, gshift.at[br], cols + side * pixels,
                    )
                for n in range(own_taps):
                    t = tap0 + n
                    start = pl.multiple_of((2 - t // 3) * cols, cols)
                    rhs = gshift[br, 2 - t % 3, pl.ds(start, 2 * pixels), :]
                    acc[br, n * ch : (n + 1) * ch, :] += jnp.dot(
                        ft[image, br], rhs, preferred_element_type=jnp.float32
                    )
            return c

        lax.fori_loop(0, replicas, one, 0)

    each_micro(weight_terms)
    out_copy = local(acc.at[:, pl.ds(offset, own)], result, 2 * micro + 3)
    out_copy.start()

    def finish(m):
        pl.when(first)(lambda: rim_send(X, m).wait_send())
        pl.when(last)(lambda: rim_send(G, m).wait_send())

        @pl.when(jnp.logical_not(last))
        def _():
            for copy in sends(X, m, yout, follow):
                copy.wait_send()
            pq_copy(m).wait_send()

        @pl.when(jnp.logical_not(first))
        def _():
            for copy in sends(G, m, sout.at[0], ahead):
                copy.wait_send()

        @pl.when(use_gskip)
        def _():
            for copy in sends(SKIP, m, yout, pair):
                copy.wait_send()

        @pl.when(use_skip)
        def _():
            for copy in sends(GSKIP, m, sout.at[1], pair):
                copy.wait_send()

        for k in range(1, peers):
            share(f_all, f_s, f_r, m, k).wait_send()
            share(g_all, g_s, g_r, m, k).wait_send()

    each_micro(finish)
    out_copy.wait()


def shards(images, timesteps, time_embed, conv_weight, norm_gain, out_grad):
    micro, rows, cols, ch = images.shape
    sections = lax.axis_size("section")
    replicas = lax.axis_size("dp")
    spaces = lax.axis_size("space")
    taps = conv_weight.shape[2]
    peers = replicas * spaces
    own = taps // peers
    own_taps = max(((n + 1) * own - 1) // ch - n * own // ch + 1 for n in range(peers))
    loss_scale = 1.0 / math.sqrt(micro * replicas * rows * spaces * cols)
    pixels = rows * cols
    frame = pixels + 2 * cols
    bf, f32 = jnp.bfloat16, jnp.float32
    dma = pltpu.SemaphoreType.DMA
    any_spec = pl.BlockSpec(memory_space=pl.ANY)
    result = pl.pallas_call(
        functools.partial(
            kernel, sections, replicas, micro, rows, cols, ch, taps, own_taps, loss_scale
        ),
        out_shape=jax.ShapeDtypeStruct((2, own, ch), f32),
        in_specs=[pl.BlockSpec(memory_space=pltpu.SMEM)] + [any_spec] * 5,
        out_specs=any_spec,
        scratch_shapes=[
            pltpu.VMEM((4, micro, frame, ch), bf),
            pltpu.VMEM((micro, 2, frame, ch), f32),
            pltpu.VMEM((micro, pixels, ch), bf),
            pltpu.VMEM((2, micro, pixels, ch), bf),
            pltpu.VMEM((micro, 2, pixels, ch), f32),
            pltpu.VMEM((2, 3, frame, ch), bf),
            pltpu.VMEM((2, taps, ch), bf),
            pltpu.VMEM((2, taps, ch), bf),
            pltpu.VMEM(time_embed.shape, f32),
            pltpu.VMEM((2, ch), f32),
            pltpu.VMEM((micro, 2, ch), f32),
            pltpu.VMEM((replicas * micro, 2, 2, pixels, ch), bf),
            pltpu.VMEM((replicas * micro, 2, 2, pixels, ch), bf),
            pltpu.VMEM((replicas * micro, 2, ch, 2 * pixels), bf),
            pltpu.VMEM((2, 3, 2 * pixels + 2 * cols, ch), bf),
            pltpu.VMEM((2, own_taps * ch, ch), f32),
            dma((2 * micro + 4,)),
            dma((4, micro)),
            dma((4, micro)),
            dma((4, micro)),
            dma((4, micro)),
            dma((micro,)),
            dma((micro,)),
            dma((peers, micro)),
            dma((peers, micro)),
            dma((peers, micro)),
            dma((peers, micro)),
        ],
        compiler_params=pltpu.CompilerParams(
            collective_id=0, has_side_effects=True, vmem_limit_bytes=48 * 2**20
        ),
    )(
        timesteps,
        images.reshape(micro, pixels, ch),
        time_embed,
        conv_weight[0],
        norm_gain[0],
        out_grad.reshape(micro, pixels, ch),
    )
    return result[None]


def solution(mesh):
    placed = (
        P(("groups", "dp"), "space", None, None),
        P(("groups", "dp")),
        P(),
        P("section", None, None, None),
        P("section", None, None),
        P(("groups", "dp"), "space", None, None),
    )
    return jax.shard_map(
        shards,
        mesh=mesh,
        in_specs=placed,
        out_specs=P(("groups", "section"), None, ("dp", "space"), None),
        check_vma=False,
    )
```

time: 382 us -> 54.1 us (0.14)
  starting transfers between devices: 163 us -> 0 us
  other arithmetic: 106 us -> 0 us
  waiting for transfers between devices: 51.7 us -> 0 us
  Pallas kernels: 0 us -> 46.8 us
  local copies, waits for them, and re-layouts: 32.1 us -> 7.04 us
  between operations: 13.4 us -> 0.02 us
  matrix products: 9.72 us -> 0 us
    ppermute x52 -> x0, starting transfers between devices: 163 us -> none  [the longest x30 106 us: passed_along(): lax.ppermute(value, axis, [(source, source + steps) for source in range(l...]
    pallas_call x0 -> x1, Pallas kernels: none -> 46.8 us  [shards(): pl.pallas_call(functools.partial(kernel, sections, replicas, micro, rows,...]
    reduce_scatter x1 -> x0, waiting for transfers between devices: 33.9 us -> none  [shards(): lax.psum_scatter(weight_terms.astype(jnp.bfloat16), ('dp', 'space'), scat...]
    add x14 -> x0, other arithmetic: 31.5 us -> none  [the longest x5 31.2 us: backward_tick(): weight_terms = weight_terms + step_terms]
    select_n x15 -> x0, other arithmetic: 25.5 us -> none  [the longest x5 8.71 us: forward_tick(): jnp.where(active, lax.dynamic_update_index_in_dim(pq_store, jnp.stack([p_...]
    convert_element_type x14 -> x0, other arithmetic: 20.1 us -> none  [the longest x5 7.88 us: routed_backward(): to_pair.astype(jnp.bfloat16)]
    ppermute x52 -> x0, waiting for transfers between devices: 17.7 us -> none  [the longest x30 11.8 us: passed_along(): lax.ppermute(value, axis, [(source, source + steps) for source in range(l...]
    another operation x24 -> x0, local copies, waits for them, and re-layouts: 17.5 us -> none
  transfers between devices with their start and end apart: 53 -> 0, of which waited for: 20 -> 0; matrix products, arithmetic and copies ran while one was open for 14% -> 0% of each run, Pallas kernels for 0% -> 0%
where the time goes in v1:
time: 54.1 us; the launch traced here: 53.8 us
  Pallas kernels  46.8 us (87%)
  local copies, waits for them, and re-layouts  7.04 us (13%)
    pallas_call x1, Pallas kernels, shards(): pl.pallas_call(functools.partial(kernel, sections, replicas, micro, rows,...  46.8 us
    unnamed x13, local copies, waits for them, and re-layouts  7.04 us

profile of v1, /device:TPU:1, one launch (start us, length us, event | category | flops | bytes accessed | tf_op | source)
XLA Modules:
  0.0 53.8 jit_solution(8108645630722801403)
XLA Ops:
  0.0 0.0 copy-start
  0.0 1.7 %copy-done = bf16[1,2,2304,256]{3,2,1,0:T(8,128)(2,1)S(1)} copy-done((bf16[1,2,2304,256]{3,2,1,0:T(8,128)(2,1)S(1)}, bf16[1,2,2304,256]{3,2,1,0:T(8,128)(2,1)}, u32[]{:S(2)}) %copy-start) | copy-done | bytes 2359320
  1.7 0.0 copy-start.1
  1.7 1.2 %copy-done.1 = f32[1000,256]{1,0:T(8,128)S(1)} copy-done((f32[1000,256]{1,0:T(8,128)S(1)}, f32[1000,256]{1,0:T(8,128)}, u32[]{:S(2)}) %copy-start.1) | copy-done | bytes 1024024
  2.9 0.0 copy-start.2
  2.9 0.9 %copy-done.2 = bf16[2,8,16,256]{3,2,1,0:T(8,128)(2,1)S(1)} copy-done((bf16[2,8,16,256]{3,2,1,0:T(8,128)(2,1)S(1)}, bf16[2,8,16,256]{3,2,1,0:T(8,128)(2,1)}, u32[]{:S(2)}) %copy-start.2) | copy-done | bytes 131096
  3.8 0.0 copy-start.3
  3.8 0.9 %copy-done.3 = bf16[2,8,16,256]{3,2,1,0:T(8,128)(2,1)S(1)} copy-done((bf16[2,8,16,256]{3,2,1,0:T(8,128)(2,1)S(1)}, bf16[2,8,16,256]{3,2,1,0:T(8,128)(2,1)}, u32[]{:S(2)}) %copy-start.3) | copy-done | bytes 131096
  4.7 0.0 copy-start.4
  4.7 0.7 %copy-done.4 = f32[1,2,256]{2,1,0:T(2,128)S(1)} copy-done((f32[1,2,256]{2,1,0:T(2,128)S(1)}, f32[1,2,256]{2,1,0:T(2,128)}, u32[]{:S(2)}) %copy-start.4) | copy-done | bytes 2072
  5.4 0.0 copy-start.5
  5.4 0.7 %copy-done.5 = s32[2]{0:T(128)S(1)} copy-done((s32[2]{0:T(128)S(1)}, s32[2]{0:T(128)}, u32[]{:S(2)}) %copy-start.5) | copy-done | bytes 32
  6.0 46.8 %shard_map.64 = f32[2,576,256]{2,1,0:T(8,128)S(1)} custom-call(s32[2]{0:T(128)S(1)} %copy-done.5, bf16[2,128,256]{2,1,0:T(8,128)(2,1)S(1)} %bitcast.7, f32[1000,256]{1,0:T(8,128)S(1)} %copy-done.1, bf16[2,2304,256]{2,1,0:T(8,128)(2,1)S(1)} %bitcast.6, f32[2,256]{1,0:T(2,128)S(1)} %bitcast.9, bf16[2,128,256]{2,1,0:T(8,128)(2,1)S(1)} %bitcast.8), custom_call_target="tpu_custom_call" | custom-call | tf_op jit(solution)/shard_map/pallas_call | solution.py:450
  52.8 1.0 %copy.8 = f32[1,2,576,256]{3,2,1,0:T(8,128)} copy(f32[1,2,576,256]{3,2,1,0:T(8,128)S(1)} %bitcast.5) | data formatting | bytes 2359296
Async XLA Ops:
  0.0 1.7 %copy-start = (bf16[1,2,2304,256]{3,2,1,0:T(8,128)(2,1)S(1)}, bf16[1,2,2304,256]{3,2,1,0:T(8,128)(2,1)}, u32[]{:S(2)}) copy-start(bf16[1,2,2304,256]{3,2,1,0:T(8,128)(2,1)} %param.9) | copy-start | bytes 7077892
  1.7 1.2 %copy-start.1 = (f32[1000,256]{1,0:T(8,128)S(1)}, f32[1000,256]{1,0:T(8,128)}, u32[]{:S(2)}) copy-start(f32[1000,256]{1,0:T(8,128)} %table.1) | copy-start | bytes 3072004
  2.9 0.9 %copy-start.2 = (bf16[2,8,16,256]{3,2,1,0:T(8,128)(2,1)S(1)}, bf16[2,8,16,256]{3,2,1,0:T(8,128)(2,1)}, u32[]{:S(2)}) copy-start(bf16[2,8,16,256]{3,2,1,0:T(8,128)(2,1)} %param.6) | copy-start | bytes 393220
  3.8 0.9 %copy-start.3 = (bf16[2,8,16,256]{3,2,1,0:T(8,128)(2,1)S(1)}, bf16[2,8,16,256]{3,2,1,0:T(8,128)(2,1)}, u32[]{:S(2)}) copy-start(bf16[2,8,16,256]{3,2,1,0:T(8,128)(2,1)} %param.11) | copy-start | bytes 393220
  4.7 0.7 %copy-start.4 = (f32[1,2,256]{2,1,0:T(2,128)S(1)}, f32[1,2,256]{2,1,0:T(2,128)}, u32[]{:S(2)}) copy-start(f32[1,2,256]{2,1,0:T(2,128)} %param.10) | copy-start | bytes 6148
  5.4 0.7 %copy-start.5 = (s32[2]{0:T(128)S(1)}, s32[2]{0:T(128)}, u32[]{:S(2)}) copy-start(s32[2]{0:T(128)} %ts_ref.1) | copy-start | bytes 28

commit v2 on v1

--- a/solution.py
+++ b/solution.py
@@ -48,9 +48,9 @@
 def kernel(
     sections, replicas, micro, rows, cols, ch, taps, own_taps, loss_scale,
     ts_ref, images, table, weight, gains, out_grad, result,
-    framed, pq, yout, sout, grad_f, shift, w, wt, tab, gn, gain_mod,
-    f_all, g_all, ft, gshift, acc,
-    lsem, band_s, band_r, halo_s, halo_r, pq_s, pq_r, f_s, f_r, g_s, g_r,
+    framed, gates, yout, sout, grad_f, shift, w, wt, tab, gn, gain_mod,
+    f_all, ab_all, g_all, ft, gshift, acc,
+    lsem, band_s, band_r, halo_s, halo_r, pq_s, pq_r, f_s, f_r, ab_s, ab_r, g_s, g_r,
 ):
     sec = lax.axis_index("section")
     d = lax.axis_index("dp")
@@ -111,7 +111,7 @@
         for kind in range(4):
             framed[kind, m, pl.ds(halo_out, cols), :] = zero_row
         for br in range(2):
-            pq[m, br, pl.ds(halo_out, cols), :] = jnp.zeros((cols, ch), jnp.float32)
+            gates[m, br, pl.ds(halo_out, cols), :] = jnp.zeros((cols, ch), jnp.float32)
     for br in range(2):
         for k in range(3):
             gshift[br, k, 0:cols, :] = zero_row
@@ -154,14 +154,14 @@
 
     def pq_copy(m):
         return pltpu.make_async_remote_copy(
-            pq.at[m, :, pl.ds(pl.multiple_of(edge + cols, cols), cols)],
-            pq.at[m, :, pl.ds(halo_out, cols)],
+            gates.at[m, :, pl.ds(pl.multiple_of(edge + cols, cols), cols)],
+            gates.at[m, :, pl.ds(halo_out, cols)],
             pq_s.at[m], pq_r.at[m], device_id={"space": other}, device_id_type=MESH,
         )
 
     def pq_wait(m):
         pltpu.make_async_remote_copy(
-            pq.at[m, :, pl.ds(cols, cols)], pq.at[m, :, pl.ds(halo_in, cols)],
+            gates.at[m, :, pl.ds(cols, cols)], gates.at[m, :, pl.ds(halo_in, cols)],
             pq_s.at[m], pq_r.at[m], device_id={"space": other}, device_id_type=MESH,
         ).wait_recv()
 
@@ -172,13 +172,18 @@
             device_id={"dp": to // 2, "space": to % 2}, device_id_type=MESH,
         )
 
-    def share_wait(ref, send, recv, m, k):
-        source = lax.rem(me - k + peers, peers)
-        slot = ref.at[source // 2 * micro + m, source % 2]
-        pltpu.make_async_remote_copy(
-            slot, slot, send.at[k, m], recv.at[k, m],
-            device_id={"dp": source // 2, "space": source % 2}, device_id_type=MESH,
-        ).wait_recv()
+    def share_wait(ref, send, recv, m, r):
+        def one(side):
+            source = r * 2 + side
+            k = lax.rem(me - source + peers, peers)
+            slot = ref.at[r * micro + m, side]
+            pltpu.make_async_remote_copy(
+                slot, slot, send.at[k, m], recv.at[k, m],
+                device_id={"dp": r, "space": side}, device_id_type=MESH,
+            ).wait_recv()
+
+        one(other)
+        pl.when(r != d)(lambda: one(h))
 
     def each_micro(body):
         lax.fori_loop(0, micro, lambda m, c: (body(m), c)[1], 0)
@@ -258,10 +263,18 @@
             for copy in sends(SKIP, m, yout, pair):
                 copy.start()
 
-        pq[m, 0, band, :] = p
-        pq[m, 1, band, :] = q
-        pq_copy(m).start()
         share_f(m)
+
+        @pl.when(enc)
+        def _():
+            slot = d * micro + m
+            s = sigmoid(q)
+            for br, gate in ((0, s), (1, p * s * (1.0 - s))):
+                gates[m, br, band, :] = gate
+                ab_all[slot, h, br, :, :] = gate.astype(jnp.bfloat16)
+            pq_copy(m).start()
+            for k in range(1, peers):
+                share(ab_all, ab_s, ab_r, m, k).start()
 
     def transposes():
         def one(t, c):
@@ -282,16 +295,14 @@
             halo_wait(GSKIP, m)
 
         g = out_gradient(m, pl.ds(0, frame))
-        s = sigmoid(pq[m, 1])
-        gp = jnp.where(enc, g * s, g)
-        gq = jnp.where(enc, g * pq[m, 0] * s * (1.0 - s), g)
-        for br, grad in ((0, gp), (1, gq)):
-            store_shifts(grad, cols, shift.at[br], 0)
-            g_all[d * micro + m, h, br, :, :] = shift[br, 1, cols : cols + pixels, :]
+        g_all[d * micro + m, h, :, :] = g[cols : cols + pixels].astype(jnp.bfloat16)
         pl.when(first)(lambda: share_g(m))
 
         @pl.when(jnp.logical_not(first))
         def _():
+            for br in range(2):
+                grad = jnp.where(enc, g * gates[m, br], g)
+                store_shifts(grad, cols, shift.at[br], 0)
             for br in range(2):
                 grad_f[m, br] = conv(wt, br, True)
 
@@ -326,10 +337,10 @@
 
     def gather_fields():
         def one(m):
-            for k in range(1, peers):
-                share_wait(f_all, f_s, f_r, m, k)
-
-            def flip(r, c):
+            def flip(rr, c):
+                r = lax.rem(d + rr, replicas)
+                share_wait(f_all, f_s, f_r, m, r)
+                pl.when(enc)(lambda: share_wait(ab_all, ab_s, ab_r, m, r))
                 for br in range(2):
                     for side in range(2):
                         at = slice(side * pixels, (side + 1) * pixels)
@@ -355,7 +366,7 @@
     def other_sections():
         each_micro(forward)
         pl.when(jnp.logical_not(first))(transposes)
-        each_micro(pq_wait)
+        pl.when(enc)(lambda: each_micro(pq_wait))
         pl.when(enc)(gather_fields)
 
         def one(m):
@@ -373,17 +384,17 @@
     offset = pl.multiple_of(me * own - tap0 * ch, 16)
 
     def weight_terms(m):
-        for k in range(1, peers):
-            share_wait(g_all, g_s, g_r, m, k)
-
-        def one(r, c):
+        def one(rr, c):
+            r = lax.rem(d + rr, replicas)
             image = r * micro + m
+            share_wait(g_all, g_s, g_r, m, r)
             for br in range(2):
                 for side in range(2):
-                    store_shifts(
-                        g_all[image, side, br].astype(jnp.float32),
-                        cols, gshift.at[br], cols + side * pixels,
-                    )
+                    g = g_all[image, side].astype(jnp.float32)
+                    gate = ab_all[image, side, br].astype(jnp.float32)
+                    grad = jnp.where(enc, g * gate, g)
+                    store_shifts(grad, cols, gshift.at[br], cols + side * pixels)
+            for br in range(2):
                 for n in range(own_taps):
                     t = tap0 + n
                     start = pl.multiple_of((2 - t // 3) * cols, cols)
@@ -407,7 +418,12 @@
         def _():
             for copy in sends(X, m, yout, follow):
                 copy.wait_send()
+
+        @pl.when(enc)
+        def _():
             pq_copy(m).wait_send()
+            for k in range(1, peers):
+                share(ab_all, ab_s, ab_r, m, k).wait_send()
 
         @pl.when(jnp.logical_not(first))
         def _():
@@ -446,7 +462,7 @@
     frame = pixels + 2 * cols
     bf, f32 = jnp.bfloat16, jnp.float32
     dma = pltpu.SemaphoreType.DMA
-    any_spec = pl.BlockSpec(memory_space=pl.ANY)
+    any_spec = pl.BlockSpec(memory_space=pltpu.HBM)
     result = pl.pallas_call(
         functools.partial(
             kernel, sections, replicas, micro, rows, cols, ch, taps, own_taps, loss_scale
@@ -468,6 +484,7 @@
             pltpu.VMEM((micro, 2, ch), f32),
             pltpu.VMEM((replicas * micro, 2, 2, pixels, ch), bf),
             pltpu.VMEM((replicas * micro, 2, 2, pixels, ch), bf),
+            pltpu.VMEM((replicas * micro, 2, pixels, ch), bf),
             pltpu.VMEM((replicas * micro, 2, ch, 2 * pixels), bf),
             pltpu.VMEM((2, 3, 2 * pixels + 2 * cols, ch), bf),
             pltpu.VMEM((2, own_taps * ch, ch), f32),
@@ -482,9 +499,11 @@
             dma((peers, micro)),
             dma((peers, micro)),
             dma((peers, micro)),
+            dma((peers, micro)),
+            dma((peers, micro)),
         ],
         compiler_params=pltpu.CompilerParams(
-            collective_id=0, has_side_effects=True, vmem_limit_bytes=48 * 2**20
+            collective_id=0, has_side_effects=True, vmem_limit_bytes=60 * 2**20
         ),
     )(
         timesteps,

time: 54.1 us -> 51 us (0.943)
  local copies, waits for them, and re-layouts: 7.04 us -> 2.36 us
  Pallas kernels: 46.8 us -> 48.5 us
    unnamed x13 -> x1, local copies, waits for them, and re-layouts: 7.04 us -> 2.36 us
    pallas_call x1, Pallas kernels: 46.8 us -> 48.5 us  [shards(): pl.pallas_call(functools.partial(kernel, sections, replicas, micro, rows,...]
where the time goes in v2:
time: 51 us; the launch traced here: 50.8 us
  Pallas kernels  48.5 us (95%)
  local copies, waits for them, and re-layouts  2.36 us (5%)
    pallas_call x1, Pallas kernels, shards(): pl.pallas_call(functools.partial(kernel, sections, replicas, micro, rows,...  48.5 us
    unnamed x1, local copies, waits for them, and re-layouts  2.36 us

profile of v2, /device:TPU:1, one launch (start us, length us, event | category | flops | bytes accessed | tf_op | source)
XLA Modules:
  0.0 50.8 jit_solution(15862841225742091657)
XLA Ops:
  0.0 48.5 %shard_map.64 = f32[2,576,256]{2,1,0:T(8,128)} custom-call(s32[2]{0:T(128)} %ts_ref.1, bf16[2,128,256]{2,1,0:T(8,128)(2,1)} %bitcast.7, f32[1000,256]{1,0:T(8,128)} %table.1, bf16[2,2304,256]{2,1,0:T(8,128)(2,1)} %bitcast.6, f32[2,256]{1,0:T(2,128)} %bitcast.9, bf16[2,128,256]{2,1,0:T(8,128)(2,1)} %bitcast.8), custom_call_target="tpu_custom_call" | custom-call | tf_op jit(solution)/shard_map/pallas_call | solution.py:466
  48.5 2.4 %copy.8 = f32[1,2,576,256]{3,2,1,0:T(8,128)} copy(f32[1,2,576,256]{3,2,1,0:T(8,128)} %bitcast.5) | data formatting | bytes 2359296

commit v3 on v2

--- a/solution.py
+++ b/solution.py
@@ -48,9 +48,11 @@
 def kernel(
     sections, replicas, micro, rows, cols, ch, taps, own_taps, loss_scale,
     ts_ref, images, table, weight, gains, out_grad, result,
-    framed, gates, yout, sout, grad_f, shift, w, wt, tab, gn, gain_mod,
+    framed, gates, yout, sout, seed, gf_in, grad_f, shift, w, wt, tab, gn, gn_last, gain_mod,
+    gain_last, ts_held,
     f_all, ab_all, g_all, ft, gshift, acc,
-    lsem, band_s, band_r, halo_s, halo_r, pq_s, pq_r, f_s, f_r, ab_s, ab_r, g_s, g_r,
+    lsem, band_s, band_r, halo_s, halo_r, pq_s, pq_r, gf_s, gf_r, gain_s, gain_r,
+    fx_s, fx_r, fh_s, fh_r, ax_s, ax_r, ah_s, ah_r, g_s, g_r,
 ):
     sec = lax.axis_index("section")
     d = lax.axis_index("dp")
@@ -59,7 +61,7 @@
     block = sec // 2
     enc = sec % 2 == 0
     dec = jnp.logical_not(enc)
-    first, last = sec == 0, sec == 1
+    first, last, pre = sec == 0, sec == 1, sec == 3
     turn = block == sections // 2 - 1
     follow = jnp.where(enc, jnp.where(turn, sec + 1, sec + 2), jnp.where(last, 0, sec - 2))
     ahead = jnp.where(dec, jnp.where(turn, sec - 1, sec + 2), jnp.where(first, 1, sec - 2))
@@ -84,12 +86,18 @@
     def seed_copy(m):
         return local(out_grad.at[m], framed.at[G, m, band], micro + m)
 
+    def pre_copy(m):
+        return local(out_grad.at[m], seed.at[m], micro + m)
+
+    ts_copy = local(ts_ref, ts_held, 2 * micro + 4)
     table_copy = local(table, tab, 2 * micro)
     gains_copy = local(gains, gn, 2 * micro + 1)
     weight_copy = local(weight, w, 2 * micro + 2)
     for m in range(micro):
         pl.when(first)(lambda m=m: image_copy(m).start())
         pl.when(last)(lambda m=m: seed_copy(m).start())
+        pl.when(pre)(lambda m=m: pre_copy(m).start())
+    ts_copy.start()
     table_copy.start()
     gains_copy.start()
     weight_copy.start()
@@ -172,6 +180,51 @@
             device_id={"dp": to // 2, "space": to % 2}, device_id_type=MESH,
         )
 
+    def across(ref, send, recv, m, k):
+        slot = ref.at[d * micro + m, h]
+        return pltpu.make_async_remote_copy(
+            slot, slot, send.at[k, m], recv.at[k, m],
+            device_id={"dp": lax.rem(d + k, replicas)}, device_id_type=MESH,
+        )
+
+    def beside(ref, send, recv, m, r, side):
+        slot = ref.at[r * micro + m, side]
+        return pltpu.make_async_remote_copy(
+            slot, slot, send.at[r, m], recv.at[r, m],
+            device_id={"space": other}, device_id_type=MESH,
+        )
+
+    def start_fields(m):
+        for k in range(1, replicas):
+            across(f_all, fx_s, fx_r, m, k).start()
+        beside(f_all, fh_s, fh_r, m, d, h).start()
+
+        @pl.when(enc)
+        def _():
+            for k in range(1, replicas):
+                across(ab_all, ax_s, ax_r, m, k).start()
+            beside(ab_all, ah_s, ah_r, m, d, h).start()
+
+    def hand_on(ref, xs, xr, hs, hr, m, r):
+        slot = ref.at[r * micro + m, h]
+        k = lax.rem(d - r + replicas, replicas)
+        pltpu.make_async_remote_copy(
+            slot, slot, xs.at[k, m], xr.at[k, m], device_id={"dp": r}, device_id_type=MESH
+        ).wait_recv()
+        beside(ref, hs, hr, m, r, h).start()
+
+    def gf_copy(m):
+        return pltpu.make_async_remote_copy(
+            sout.at[0, m], gf_in.at[m], gf_s.at[m], gf_r.at[m],
+            device_id={"section": ahead}, device_id_type=MESH,
+        )
+
+    def gain_copy():
+        return pltpu.make_async_remote_copy(
+            gn, gn_last, gain_s.at[0], gain_r.at[0],
+            device_id={"section": ahead}, device_id_type=MESH,
+        )
+
     def share_wait(ref, send, recv, m, r):
         def one(side):
             source = r * 2 + side
@@ -201,20 +254,25 @@
         pl.when(last)(lambda: each_micro(seeds_in))
 
     start_rims()
+    gains_copy.wait()
+    pl.when(last)(lambda: gain_copy().start())
+    ts_copy.wait()
     table_copy.wait()
-    gains_copy.wait()
+
+    def modulation(m):
+        return 1.0 + tab[pl.ds(ts_held[m], 1), :]
+
     for m in range(micro):
-        modulation = 1.0 + tab[pl.ds(ts_ref[m], 1), :]
-        gain_mod[m, :, :] = gn[...] * modulation
-    weight_copy.wait()
+        gain_mod[m, :, :] = gn[...] * modulation(m)
 
     def gain_of(m, br):
         return gain_mod[m, pl.ds(br, 1), :]
 
-    def wait_inputs(m):
+    def wait_x(m):
         pl.when(jnp.logical_not(first))(lambda: band_wait(X, m))
         halo_wait(X, m)
 
+    def wait_skip(m):
         @pl.when(use_skip)
         def _():
             band_wait(SKIP, m)
@@ -224,10 +282,6 @@
         a = framed[X, m, part, :].astype(jnp.float32)
         v = jnp.where(use_skip, framed[SKIP, m, part, :].astype(jnp.float32), a)
         return a, v
-
-    def share_f(m):
-        for k in range(1, peers):
-            share(f_all, f_s, f_r, m, k).start()
 
     def share_g(m):
         for k in range(1, peers):
@@ -244,17 +298,30 @@
         return jnp.dot(lhs, kernels[br], preferred_element_type=jnp.float32)
 
     def forward(m):
-        wait_inputs(m)
+        wait_skip(m)
+        wait_x(m)
         a, v = inputs(m, pl.ds(0, frame))
         for br, x in ((0, a), (1, v)):
             f = normalize(x, gain_of(m, br))
             store_shifts(f, cols, shift.at[br], 0)
             f_all[d * micro + m, h, br, :, :] = shift[br, 1, cols : cols + pixels, :]
+        pl.when(jnp.logical_and(enc, m == 0))(weight_copy.wait)
         p = conv(w, 0, False)
         q = conv(w, 1, False)
         centre = framed[X, m, band, :].astype(jnp.float32)
         y = jnp.where(enc, centre + p * sigmoid(q), centre + p + q)
         yout[m] = y.astype(jnp.bfloat16)
+
+        @pl.when(pre)
+        def _():
+            gf_copy(m).wait_recv()
+            pre_copy(m).wait()
+            x = yout[m].astype(jnp.float32)
+            main = pull_back(x, gain_last[m, 0:1, :], gf_in[m].astype(jnp.float32))
+            grad = seed[m].astype(jnp.float32) * loss_scale + main
+            framed[G, m, band, :] = grad.astype(jnp.bfloat16)
+            rim_send(G, m).start()
+
         for copy in sends(X, m, yout, follow):
             copy.start()
 
@@ -262,8 +329,6 @@
         def _():
             for copy in sends(SKIP, m, yout, pair):
                 copy.start()
-
-        share_f(m)
 
         @pl.when(enc)
         def _():
@@ -273,8 +338,6 @@
                 gates[m, br, band, :] = gate
                 ab_all[slot, h, br, :, :] = gate.astype(jnp.bfloat16)
             pq_copy(m).start()
-            for k in range(1, peers):
-                share(ab_all, ab_s, ab_r, m, k).start()
 
     def transposes():
         def one(t, c):
@@ -286,7 +349,7 @@
         lax.fori_loop(0, 9, one, 0)
 
     def field_grads(m):
-        pl.when(jnp.logical_not(last))(lambda: band_wait(G, m))
+        pl.when(jnp.logical_not(jnp.logical_or(last, pre)))(lambda: band_wait(G, m))
         halo_wait(G, m)
 
         @pl.when(use_gskip)
@@ -329,18 +392,33 @@
 
         share_g(m)
 
+    def last_skip(m):
+        wait_skip(m)
+        v = framed[SKIP, m, band, :].astype(jnp.float32)
+        sout[1, m] = pull_back(v, gain_of(m, 1), grad_f[m, 1]).astype(jnp.bfloat16)
+        for copy in sends(GSKIP, m, sout.at[1], pair):
+            copy.start()
+
     def late_fields(m):
+        wait_x(m)
         a, v = inputs(m, band)
         for br, x in ((0, a), (1, v)):
             f_all[d * micro + m, h, br, :, :] = normalize(x, gain_of(m, br)).astype(jnp.bfloat16)
-        share_f(m)
 
     def gather_fields():
         def one(m):
+            def pass_on(rr, c):
+                r = lax.rem(d + rr, replicas)
+                hand_on(f_all, fx_s, fx_r, fh_s, fh_r, m, r)
+                pl.when(enc)(lambda: hand_on(ab_all, ax_s, ax_r, ah_s, ah_r, m, r))
+                return c
+
+            lax.fori_loop(1, replicas, pass_on, 0)
+
             def flip(rr, c):
                 r = lax.rem(d + rr, replicas)
-                share_wait(f_all, f_s, f_r, m, r)
-                pl.when(enc)(lambda: share_wait(ab_all, ab_s, ab_r, m, r))
+                beside(f_all, fh_s, fh_r, m, r, other).wait_recv()
+                pl.when(enc)(lambda: beside(ab_all, ah_s, ah_r, m, r, other).wait_recv())
                 for br in range(2):
                     for side in range(2):
                         at = slice(side * pixels, (side + 1) * pixels)
@@ -352,29 +430,52 @@
         each_micro(one)
 
     def last_section():
+        weight_copy.wait()
         transposes()
-        each_micro(field_grads)
 
         def one(m):
-            wait_inputs(m)
-            pass_grads(m)
+            field_grads(m)
+            sout[0, m] = grad_f[m, 0].astype(jnp.bfloat16)
+            gf_copy(m).start()
 
         each_micro(one)
+        each_micro(last_skip)
+        each_micro(share_g)
         each_micro(late_fields)
+        each_micro(start_fields)
         gather_fields()
 
     def other_sections():
+        @pl.when(dec)
+        def _():
+            weight_copy.wait()
+            transposes()
+
+        @pl.when(pre)
+        def _():
+            gain_copy().wait_recv()
+            for m in range(micro):
+                gain_last[m, :, :] = gn_last[...] * modulation(m)
+
         each_micro(forward)
-        pl.when(jnp.logical_not(first))(transposes)
-        pl.when(enc)(lambda: each_micro(pq_wait))
-        pl.when(enc)(gather_fields)
+
+        @pl.when(enc)
+        def _():
+            each_micro(start_fields)
+            pl.when(jnp.logical_not(first))(transposes)
+            each_micro(pq_wait)
+            gather_fields()
 
         def one(m):
             field_grads(m)
             pl.when(jnp.logical_not(first))(lambda: pass_grads(m))
 
         each_micro(one)
-        pl.when(dec)(gather_fields)
+
+        @pl.when(dec)
+        def _():
+            each_micro(start_fields)
+            gather_fields()
 
     pl.when(last)(last_section)
     pl.when(jnp.logical_not(last))(other_sections)
@@ -412,7 +513,8 @@
 
     def finish(m):
         pl.when(first)(lambda: rim_send(X, m).wait_send())
-        pl.when(last)(lambda: rim_send(G, m).wait_send())
+        pl.when(jnp.logical_or(last, pre))(lambda: rim_send(G, m).wait_send())
+        pl.when(last)(lambda: gf_copy(m).wait_send())
 
         @pl.when(jnp.logical_not(last))
         def _():
@@ -422,10 +524,12 @@
         @pl.when(enc)
         def _():
             pq_copy(m).wait_send()
-            for k in range(1, peers):
-                share(ab_all, ab_s, ab_r, m, k).wait_send()
-
-        @pl.when(jnp.logical_not(first))
+            for k in range(1, replicas):
+                across(ab_all, ax_s, ax_r, m, k).wait_send()
+            for r in range(replicas):
+                beside(ab_all, ah_s, ah_r, m, r, h).wait_send()
+
+        @pl.when(jnp.logical_not(jnp.logical_or(first, last)))
         def _():
             for copy in sends(G, m, sout.at[0], ahead):
                 copy.wait_send()
@@ -441,10 +545,14 @@
                 copy.wait_send()
 
         for k in range(1, peers):
-            share(f_all, f_s, f_r, m, k).wait_send()
             share(g_all, g_s, g_r, m, k).wait_send()
+        for k in range(1, replicas):
+            across(f_all, fx_s, fx_r, m, k).wait_send()
+        for r in range(replicas):
+            beside(f_all, fh_s, fh_r, m, r, h).wait_send()
 
     each_micro(finish)
+    pl.when(last)(lambda: gain_copy().wait_send())
     out_copy.wait()
 
 
@@ -462,43 +570,56 @@
     frame = pixels + 2 * cols
     bf, f32 = jnp.bfloat16, jnp.float32
     dma = pltpu.SemaphoreType.DMA
-    any_spec = pl.BlockSpec(memory_space=pltpu.HBM)
+    hbm_spec = pl.BlockSpec(memory_space=pltpu.HBM)
     result = pl.pallas_call(
         functools.partial(
             kernel, sections, replicas, micro, rows, cols, ch, taps, own_taps, loss_scale
         ),
         out_shape=jax.ShapeDtypeStruct((2, own, ch), f32),
-        in_specs=[pl.BlockSpec(memory_space=pltpu.SMEM)] + [any_spec] * 5,
-        out_specs=any_spec,
+        in_specs=[hbm_spec] * 6,
+        out_specs=pl.BlockSpec(memory_space=pl.ANY),
         scratch_shapes=[
             pltpu.VMEM((4, micro, frame, ch), bf),
             pltpu.VMEM((micro, 2, frame, ch), f32),
             pltpu.VMEM((micro, pixels, ch), bf),
             pltpu.VMEM((2, micro, pixels, ch), bf),
+            pltpu.VMEM((micro, pixels, ch), bf),
+            pltpu.VMEM((micro, pixels, ch), bf),
             pltpu.VMEM((micro, 2, pixels, ch), f32),
             pltpu.VMEM((2, 3, frame, ch), bf),
             pltpu.VMEM((2, taps, ch), bf),
             pltpu.VMEM((2, taps, ch), bf),
             pltpu.VMEM(time_embed.shape, f32),
             pltpu.VMEM((2, ch), f32),
+            pltpu.VMEM((2, ch), f32),
             pltpu.VMEM((micro, 2, ch), f32),
+            pltpu.VMEM((micro, 2, ch), f32),
+            pltpu.SMEM((micro,), jnp.int32),
             pltpu.VMEM((replicas * micro, 2, 2, pixels, ch), bf),
             pltpu.VMEM((replicas * micro, 2, 2, pixels, ch), bf),
             pltpu.VMEM((replicas * micro, 2, pixels, ch), bf),
             pltpu.VMEM((replicas * micro, 2, ch, 2 * pixels), bf),
             pltpu.VMEM((2, 3, 2 * pixels + 2 * cols, ch), bf),
             pltpu.VMEM((2, own_taps * ch, ch), f32),
-            dma((2 * micro + 4,)),
+            dma((2 * micro + 5,)),
             dma((4, micro)),
             dma((4, micro)),
             dma((4, micro)),
             dma((4, micro)),
             dma((micro,)),
             dma((micro,)),
-            dma((peers, micro)),
-            dma((peers, micro)),
-            dma((peers, micro)),
-            dma((peers, micro)),
+            dma((micro,)),
+            dma((micro,)),
+            dma((1,)),
+            dma((1,)),
+            dma((replicas, micro)),
+            dma((replicas, micro)),
+            dma((replicas, micro)),
+            dma((replicas, micro)),
+            dma((replicas, micro)),
+            dma((replicas, micro)),
+            dma((replicas, micro)),
+            dma((replicas, micro)),
             dma((peers, micro)),
             dma((peers, micro)),
         ],

time: 51 us -> 44.3 us (0.87)
  Pallas kernels: 48.5 us -> 41.8 us
    pallas_call x1, Pallas kernels: 48.5 us -> 41.8 us  [shards(): pl.pallas_call(functools.partial(kernel, sections, replicas, micro, rows,...]
where the time goes in v3:
time: 44.3 us; the launch traced here: 44.2 us
  Pallas kernels  41.8 us (94%)
  local copies, waits for them, and re-layouts  2.36 us (5%)
    pallas_call x1, Pallas kernels, shards(): pl.pallas_call(functools.partial(kernel, sections, replicas, micro, rows,...  41.8 us
    unnamed x1, local copies, waits for them, and re-layouts  2.36 us

profile of v3, /device:TPU:1, one launch (start us, length us, event | category | flops | bytes accessed | tf_op | source)
XLA Modules:
  0.0 44.2 jit_solution(9939956983502407112)
XLA Ops:
  0.0 41.8 %shard_map.64 = f32[2,576,256]{2,1,0:T(8,128)} custom-call(s32[2]{0:T(128)} %ts_ref.1, bf16[2,128,256]{2,1,0:T(8,128)(2,1)} %bitcast.7, f32[1000,256]{1,0:T(8,128)} %table.1, bf16[2,2304,256]{2,1,0:T(8,128)(2,1)} %bitcast.6, f32[2,256]{1,0:T(2,128)} %bitcast.9, bf16[2,128,256]{2,1,0:T(8,128)(2,1)} %bitcast.8), custom_call_target="tpu_custom_call" | custom-call | tf_op jit(solution)/shard_map/pallas_call | solution.py:574
  41.8 2.4 %copy.8 = f32[1,2,576,256]{3,2,1,0:T(8,128)} copy(f32[1,2,576,256]{3,2,1,0:T(8,128)} %bitcast.5) | data formatting | bytes 2359296

commit v4 on v3

--- a/solution.py
+++ b/solution.py
@@ -325,11 +325,6 @@
         for copy in sends(X, m, yout, follow):
             copy.start()
 
-        @pl.when(use_gskip)
-        def _():
-            for copy in sends(SKIP, m, yout, pair):
-                copy.start()
-
         @pl.when(enc)
         def _():
             slot = d * micro + m
@@ -338,6 +333,12 @@
                 gates[m, br, band, :] = gate
                 ab_all[slot, h, br, :, :] = gate.astype(jnp.bfloat16)
             pq_copy(m).start()
+
+    def send_skip(m):
+        @pl.when(use_gskip)
+        def _():
+            for copy in sends(SKIP, m, yout, pair):
+                copy.start()
 
     def transposes():
         def one(t, c):
@@ -390,7 +391,6 @@
             for copy in sends(GSKIP, m, sout.at[1], pair):
                 copy.start()
 
-        share_g(m)
 
     def last_skip(m):
         wait_skip(m)
@@ -461,6 +461,7 @@
 
         @pl.when(enc)
         def _():
+            each_micro(send_skip)
             each_micro(start_fields)
             pl.when(jnp.logical_not(first))(transposes)
             each_micro(pq_wait)
@@ -471,6 +472,7 @@
             pl.when(jnp.logical_not(first))(lambda: pass_grads(m))
 
         each_micro(one)
+        pl.when(jnp.logical_not(first))(lambda: each_micro(share_g))
 
         @pl.when(dec)
         def _():

time: 44.3 us -> 42.8 us (0.966)
  Pallas kernels: 41.8 us -> 40.3 us
    pallas_call x1, Pallas kernels: 41.8 us -> 40.3 us  [shards(): pl.pallas_call(functools.partial(kernel, sections, replicas, micro, rows,...]
where the time goes in v4:
time: 42.8 us; the launch traced here: 42.7 us
  Pallas kernels  40.3 us (94%)
  local copies, waits for them, and re-layouts  2.36 us (6%)
    pallas_call x1, Pallas kernels, shards(): pl.pallas_call(functools.partial(kernel, sections, replicas, micro, rows,...  40.3 us
    unnamed x1, local copies, waits for them, and re-layouts  2.36 us

profile of v4, /device:TPU:1, one launch (start us, length us, event | category | flops | bytes accessed | tf_op | source)
XLA Modules:
  0.0 42.7 jit_solution(13546603169883222727)
XLA Ops:
  0.0 40.3 %shard_map.64 = f32[2,576,256]{2,1,0:T(8,128)} custom-call(s32[2]{0:T(128)} %ts_ref.1, bf16[2,128,256]{2,1,0:T(8,128)(2,1)} %bitcast.7, f32[1000,256]{1,0:T(8,128)} %table.1, bf16[2,2304,256]{2,1,0:T(8,128)(2,1)} %bitcast.6, f32[2,256]{1,0:T(2,128)} %bitcast.9, bf16[2,128,256]{2,1,0:T(8,128)(2,1)} %bitcast.8), custom_call_target="tpu_custom_call" | custom-call | tf_op jit(solution)/shard_map/pallas_call | solution.py:576
  40.3 2.4 %copy.8 = f32[1,2,576,256]{3,2,1,0:T(8,128)} copy(f32[1,2,576,256]{3,2,1,0:T(8,128)} %bitcast.5) | data formatting | bytes 2359296
